TPU v7x, 32 devices: a whole 2x2x4 slice. The times are simulated.
32 devices in a mesh: vgroup: 2 (over x), feat: 16 (over z, y, core).
Axes of the slice: x: 2, y: 2, z: 4, core: 2. Of those that a mesh axis runs over, the one named last changes fastest.
Arguments:
- features_t: bfloat16 [2, 1024, 16384], P('vgroup', 'feat'), may hold values from -6 to 6
- tile_weights: bfloat16 [2, 512, 128, 128], P('vgroup'), may hold values from -0.1875 to 0.1875
- tile_dst: int32 [2, 512], P('vgroup'), may hold values from 0 to 63
- tile_src: int32 [2, 512], P('vgroup'), may hold values from 0 to 127
- tile_count: int32 [2], P('vgroup'), may hold values from 128 to 512, as said below
- w_self: bfloat16 [1024, 256], P('feat'), may hold values from -0.1875 to 0.1875
- w_neigh: bfloat16 [1024, 256], P('feat'), may hold values from -0.1875 to 0.1875
- bias: float32 [256], replicated, may hold values from -4 to 4
- grad_hidden: bfloat16 [16384, 256], P(('vgroup', 'feat')), may hold values from -1 to 1
Outputs:
- hidden: bfloat16 [16384, 256], P(('vgroup', 'feat'))
- grad_self: float32 [1024, 256], P('feat')
- grad_neigh: float32 [1024, 256], P('feat')
- grad_bias: float32 [256], replicated
Inputs may be any that keep to these rules, and one draw needn't show every extreme that they name: `tile_count`: slots at or past a group's count are ignored; at least one group has all 512 slots live.
All inputs are finite; a program needn't handle non-finite values.
Results may differ from a plain program's by a relative error of at most 0.0075.
Values may be sent and summed in bfloat16 or wider, within the bound.
A program may use at most 192 MiB of HBM per device.

v0:
```python
import jax
import jax.numpy as jnp
from jax import lax
from jax.sharding import PartitionSpec as P


def activate(pre):
    return jax.nn.gelu(pre, approximate=True)


def left_product(columns, weights):
    return lax.dot_general(
        columns, weights, (((0,), (0,)), ((), ())), preferred_element_type=jnp.float32
    )


def gathered_grads(delta, target_columns, aggregated):
    piece = lax.all_gather(delta, "feat", axis=0, tiled=True)
    grad_s = jnp.dot(target_columns, piece, preferred_element_type=jnp.float32)
    grad_n = jnp.dot(aggregated, piece, preferred_element_type=jnp.float32)
    grad_self, grad_neigh = lax.psum((grad_s, grad_n), "vgroup")
    grad_bias = lax.psum(jnp.sum(delta, axis=0, dtype=jnp.float32), ("vgroup", "feat"))
    return (grad_self, grad_neigh, grad_bias)


def body(
    features_t, tile_weights, tile_dst, tile_src, tile_count, w_self, w_neigh, bias, grad_hidden
):
    feats = features_t[0]
    tile_list = tile_weights[0]
    dsts = tile_dst[0]
    srcs = tile_src[0]
    count = tile_count[0]
    fcols, nsrc = feats.shape
    slot_total, tile_extent = (tile_list.shape[0], tile_list.shape[1])
    nfeat = lax.axis_size("feat")
    rows_dev = grad_hidden.shape[0]
    ndst = rows_dev * nfeat
    dtiles = ndst // tile_extent
    stiles = nsrc // tile_extent
    source_blocks = feats.reshape(fcols, stiles, tile_extent)
    picked = jnp.take(source_blocks, srcs, axis=1)
    product = jnp.einsum("ftk,tjk->ftj", picked, tile_list, preferred_element_type=jnp.float32)
    slot_indices = jnp.arange(slot_total)
    live = (slot_indices < count).astype(jnp.float32)
    onehot = (dsts[None, :] == jnp.arange(dtiles)[:, None]).astype(jnp.float32) * live[None, :]
    summed = jnp.einsum("dt,ftj->fdj", onehot, product, precision=lax.Precision.HIGHEST)
    aggregated = summed.reshape(fcols, ndst).astype(jnp.bfloat16)
    target_columns = feats[:, :ndst]
    pre = (
        lax.psum_scatter(
            left_product(target_columns, w_self) + left_product(aggregated, w_neigh),
            "feat",
            scatter_dimension=0,
            tiled=True,
        )
        + bias
    )
    output, pullback = jax.vjp(activate, pre)
    delta = pullback(grad_hidden.astype(jnp.float32))[0].astype(jnp.bfloat16)
    grad_self, grad_neigh, grad_bias = gathered_grads(delta, target_columns, aggregated)
    hidden = output.astype(jnp.bfloat16)
    return (hidden, grad_self, grad_neigh, grad_bias)


def solution(mesh):
    return jax.shard_map(
        body,
        mesh=mesh,
        in_specs=(
            P("vgroup", "feat", None),
            P("vgroup", None, None, None),
            P("vgroup", None),
            P("vgroup", None),
            P("vgroup"),
            P("feat", None),
            P("feat", None),
            P(),
            P(("vgroup", "feat"), None),
        ),
        out_specs=(P(("vgroup", "feat"), None), P("feat", None), P("feat", None), P()),
        check_vma=False,
    )
```

profile of v0, /device:TPU:0, one launch (start us, length us, event | category | flops | bytes accessed | tf_op | source)
XLA Modules:
  0.0 294.9 jit_solution(14697708014028177900)
XLA Ops:
  7.2 0.0 copy-start
  7.2 0.0 reduce-scatter.2.cloned.1.call-start
  7.2 2.2 copy.15
  9.4 1.4 copy.13
  11.5 13.5 %gather_fusion = bf16[512,64,128]{2,1,0:T(8,128)(2,1)} fusion(bf16[64,128,128]{2,0,1:T(8,128)(2,1)S(1)} %copy.13, s32[1024]{0:T(1024)S(1)} %pad_clamp_fusion), kind=kCustom, calls=%fused_computation | custom fusion | bytes 16779264 | tf_op jit(solution)/shard_map/jit(_take)/gather | solution.py:42
  25.0 2.5 fusion.20
  27.5 0.0 copy-start.6
  27.5 20.5 %fusion.4 = f32[64,512,128]{2,0,1:T(8,128)} fusion(bf16[1,512,128,128]{3,2,1,0:T(8,128)(2,1)} %param.10, bf16[512,64,128]{2,1,0:T(8,128)(2,1)} %gather_fusion, pred[512]{0:T(512)(128)(4,1)S(1)} %compare_and_fusion), kind=kOutput, calls=%fused_computation.6 | convolution fusion | flops 1077936128 | bytes 41943552 | tf_op jit(solution)/shard_map/ftk,tjk->ftj/dot_general | solution.py:43
  48.0 25.4 %fusion.11 = bf16[64,128,64]{1,2,0:T(8,128)(2,1)S(1)} fusion(f32[64,512,128]{2,0,1:T(8,128)} %fusion.4, f32[512]{0:T(512)S(1)} %fusion.37, s32[512]{0:T(512)S(1)} %bitcast.45), kind=kOutput, calls=%fused_computation.11 | convolution fusion | flops 3221815296 | bytes 17829888 | tf_op jit(solution)/shard_map/dt,ftj->fdj/dot_general | solution.py:47
  73.4 5.1 %convolution_add_fusion = f32[8192,256]{1,0:T(8,128)} fusion(f32[8192,256]{1,0:T(8,128)S(1)} %fusion.20, bf16[64,256]{1,0:T(8,128)(2,1)S(1)} %copy-done.4, bf16[8,8,64,128]{3,2,1,0:T(8,128)(2,1)S(1)} %bitcast.40), kind=kOutput, calls=%fused_computation.5 | convolution fusion | flops 270532608 | bytes 17858560 | tf_op jit(solution)/shard_map/dot_general | solution.py:12
  78.5 0.0 reduce-scatter.2.cloned.1.call-update
  78.5 0.0 copy-start.1
  78.5 0.0 all-gather.2.cloned.1.call-start
  78.5 107.5 %reduce-scatter.2.cloned.1.call-done = f32[512,256]{1,0:T(8,128)} async-done(((f32[8192,256]{1,0:T(8,128)}), f32[512,256]{1,0:T(8,128)}) %reduce-scatter.2.cloned.1.call-update) | async-done | bytes 524304 | tf_op jit(solution)/shard_map/reduce_scatter | solution.py:51
  186.0 2.3 convert_reduce_fusion
  188.3 0.0 all-gather.2.cloned.1.call-update
  188.3 0.0 all-reduce.3.cloned.1.call-start
  188.3 50.4 %all-gather.2.cloned.1.call-done = bf16[8192,256]{1,0:T(8,128)(2,1)} async-done(((bf16[512,256]{1,0:T(8,128)(2,1)}), bf16[8192,256]{1,0:T(8,128)(2,1)}) %all-gather.2.cloned.1.call-update) | async-done | bytes 4194320 | tf_op jit(solution)/shard_map/all_gather | solution.py:18
  238.8 3.8 %fusion.14 = f32[64,256]{1,0:T(8,128)} fusion(bf16[8192,256]{1,0:T(8,128)(2,1)} %all-gather.2.cloned.1.call-done, bf16[8,8,64,128]{3,2,1,0:T(8,128)(2,1)S(1)} %bitcast.41), kind=kOutput, calls=%fused_computation.13 | convolution fusion | flops 268435456 | bytes 5308416 | tf_op jit(solution)/shard_map/dot_general | solution.py:20
  242.6 3.6 %convolution_bitcast_fusion = f32[64,256]{1,0:T(8,128)} fusion(bf16[8192,256]{1,0:T(8,128)(2,1)} %all-gather.2.cloned.1.call-done, bf16[64,16384]{1,0:T(8,128)(2,1)S(1)} %bitcast.39), kind=kOutput, calls=%fused_computation.12 | convolution fusion | flops 268435456 | bytes 5308416 | tf_op jit(solution)/shard_map/dot_general | solution.py:19
  246.2 0.0 all-reduce.3.cloned.1.call-update
  246.2 39.3 %psum.23 = f32[256]{0:T(256)} all-reduce(f32[256]{0:T(256)S(1)} %get-tuple-element.6), channel_id=1, replica_groups=mesh['vgroup'=2,'feat'=16] {'vgroup','feat'}, use_global_device_ids=true, to_apply=%region_4.5 | all-reduce | flops 256 | bytes 2048 | tf_op jit(solution)/shard_map/psum | solution.py:22
  285.5 1.5 copy.32
  286.9 1.5 copy.33
  (18 shorter events, 0.0 us)
Async XLA Ops:
  7.2 17.8 %copy-start = (bf16[64,256]{1,0:T(8,128)(2,1)S(1)}, bf16[64,256]{1,0:T(8,128)(2,1)}, u32[]{:S(2)}) copy-start(bf16[64,256]{1,0:T(8,128)(2,1)} %param.14) | copy-start | bytes 98308
  7.2 3.6 %copy-start.5 = (s32[1,512]{1,0:T(1,128)S(1)}, s32[1,512]{1,0:T(1,128)}, u32[]{:S(2)}) copy-start(s32[1,512]{1,0:T(1,128)} %param.12) | copy-start | bytes 6148
  7.2 178.8 %reduce-scatter.2.cloned.1.call-start = ((), (), s32[]{:S(2)}) async-start(), calls=%async_computation.1 | async-start | bytes 8912896 | tf_op jit(solution)/shard_map/reduce_scatter | solution.py:51
  27.5 20.5 %copy-start.6 = (s32[1,512]{1,0:T(1,128)S(1)}, s32[1,512]{1,0:T(1,128)}, u32[]{:S(2)}) copy-start(s32[1,512]{1,0:T(1,128)} %param.11) | copy-start | bytes 6148
  48.0 25.4 %copy-start.4 = (bf16[64,256]{1,0:T(8,128)(2,1)S(1)}, bf16[64,256]{1,0:T(8,128)(2,1)}, u32[]{:S(2)}) copy-start(bf16[64,256]{1,0:T(8,128)(2,1)} %param.15) | copy-start | bytes 98308
  78.5 107.5 %copy-start.3 = (bf16[512,256]{1,0:T(8,128)(2,1)S(1)}, bf16[512,256]{1,0:T(8,128)(2,1)}, u32[]{:S(2)}) copy-start(bf16[512,256]{1,0:T(8,128)(2,1)} %param.17) | copy-start | bytes 786436
  78.5 107.5 %copy-start.7 = (f32[256]{0:T(256)S(1)}, f32[256]{0:T(256)}, u32[]{:S(2)}) copy-start(f32[256]{0:T(256)} %param.16) | copy-start | bytes 3076
  78.5 164.1 %copy-start.2 = (bf16[1,64,16384]{2,1,0:T(8,128)(2,1)S(1)}, bf16[1,64,16384]{2,1,0:T(8,128)(2,1)}, u32[]{:S(2)}) copy-start(bf16[1,64,16384]{2,1,0:T(8,128)(2,1)} %param.9) | copy-start | bytes 6291460
  78.5 209.9 %copy-start.1 = (bf16[64,256]{1,0:T(8,128)(2,1)S(1)}, bf16[64,256]{1,0:T(8,128)(2,1)}, u32[]{:S(2)}) copy-start(bf16[64,256]{1,0:T(8,128)(2,1)} %param.14) | copy-start | bytes 98308
  78.5 160.3 %all-gather.2.cloned.1.call-start = ((), (), s32[]{:S(2)}) async-start(), calls=%async_computation.2 | async-start | bytes 4456448 | tf_op jit(solution)/shard_map/all_gather | solution.py:18
  188.3 97.2 %all-reduce.3.cloned.1.call-start = ((), (), s32[]{:S(2)}) async-start(), calls=%async_computation.3 | async-start | bytes 262144 | tf_op jit(solution)/shard_map/psum | solution.py:21
Sparse Core Ops, SparseCore 0:
  78.6 107.3 reduce-scatter.1
  188.4 50.3 all-gather.1
  246.3 20.2 all-reduce.2
where the time goes:
time: 295 us
  waiting for transfers between devices  158 us (54%)
  matrix products  60.8 us (21%)
  blocking collectives  39.3 us (13%)
  local copies, waits for them, and re-layouts  20 us (7%)
  between operations  14.5 us (5%)
    reduce_scatter x1, waiting for transfers between devices, body(): lax.psum_scatter(left_product(target_columns, w_self) + left_product(aggr...  107 us
    all_gather x1, waiting for transfers between devices, gathered_grads(): piece = lax.all_gather(delta, 'feat', axis=0, tiled=True)  50.4 us
    psum x1, blocking collectives, gathered_grads(): lax.psum(jnp.sum(delta, axis=0, dtype=jnp.float32), ('vgroup', 'feat'))  39.3 us
    dot_general x1, matrix products, body(): jnp.einsum('dt,ftj->fdj', onehot, product, precision=lax.Precision.HIGHEST)  25.4 us
    dot_general x1, matrix products, body(): jnp.einsum('ftk,tjk->ftj', picked, tile_list, preferred_element_type=jnp....  20.5 us
    gather x1, local copies, waits for them, and re-layouts, body(): picked = jnp.take(source_blocks, srcs, axis=1)  13.5 us
    dot_general x2, matrix products, left_product(): lax.dot_general(columns, weights, (((0,), (0,)), ((), ())), preferred_ele...  7.59 us
  transfers between devices with their start and end apart: 3, of which 2 were waited for; matrix products, arithmetic and copies ran while one was open for 0% of the time, Pallas kernels for 0%

commit v1 on v0

v1 whole, which is shorter than its diff:
```python
import functools

import jax
import jax.numpy as jnp
from jax import lax
from jax.experimental import pallas as pl
from jax.experimental.pallas import tpu as pltpu
from jax.sharding import PartitionSpec as P

STEP = 64
UNROLL = 8


def aggregate_kernel(dst_ref, src_ref, count_ref, x_ref, w_ref, out_ref, acc_ref):
    step = pl.program_id(0)
    tile = w_ref.shape[1]
    dtiles = out_ref.shape[1] // tile

    @pl.when(step == 0)
    def _():
        acc_ref[...] = jnp.zeros_like(acc_ref)

    @pl.loop(0, STEP // UNROLL)
    def _(group):
        for k in range(UNROLL):
            i = group * UNROLL + k
            t = step * STEP + i
            d = jnp.where(t < count_ref[0], dst_ref[t], dtiles)
            s = pl.multiple_of(src_ref[t] * tile, tile)
            prod = lax.dot_general(
                x_ref[:, pl.ds(s, tile)], w_ref[i], (((1,), (1,)), ((), ())),
                preferred_element_type=jnp.float32,
            )
            acc_ref[d] = acc_ref[d] + prod

    @pl.when(step == pl.num_programs(0) - 1)
    def _():
        for d in range(dtiles):
            out_ref[:, d * tile:(d + 1) * tile] = acc_ref[d].astype(out_ref.dtype)


def aggregate(feats, tiles, dsts, srcs, count, ndst):
    fcols, nsrc = feats.shape
    total, tile, _ = tiles.shape
    return pl.pallas_call(
        aggregate_kernel,
        grid_spec=pltpu.PrefetchScalarGridSpec(
            num_scalar_prefetch=3,
            grid=(total // STEP,),
            in_specs=[
                pl.BlockSpec((fcols, nsrc), lambda i, *_: (0, 0), pipeline_mode=pl.Buffered(1)),
                pl.BlockSpec((STEP, tile, tile), lambda i, *_: (i, 0, 0)),
            ],
            out_specs=pl.BlockSpec((fcols, ndst), lambda i, *_: (0, 0), pipeline_mode=pl.Buffered(1)),
            scratch_shapes=[pltpu.VMEM((ndst // tile + 1, fcols, tile), jnp.float32)],
        ),
        out_shape=jax.ShapeDtypeStruct((fcols, ndst), jnp.bfloat16),
        compiler_params=pltpu.CompilerParams(vmem_limit_bytes=40 * 2**20),
        cost_estimate=pl.CostEstimate(
            flops=2 * total * fcols * tile * tile, bytes_accessed=total * tile * tile * 2,
            transcendentals=0,
        ),
        name="aggregate",
    )(dsts, srcs, count, feats, tiles)


MERGE = 8
CUBIC = 0.044715
ROOT = 0.7978845608


def exchange_kernel(
    groups, nfeat,
    x_ref, a_ref, ws_ref, wn_ref, bias_ref, up_ref,
    hidden_ref, gs_ref, gn_ref, gb_ref,
    xm, am, wm, psend, precv, dall, gacc, gsend, grecv, vsend, vrecv,
    x_sems, a_sems, w_sems, p_sems, d_sems, g_sems, v_sems, l_sems,
):
    outer = nfeat // MERGE
    fcols = ws_ref.shape[0]
    rows = up_ref.shape[0]
    width = up_ref.shape[1]
    grp = lax.axis_index("vgroup")
    me = lax.axis_index("feat")
    lo = lax.rem(me, MERGE)
    hi = lax.div(me, MERGE)

    def inner_peer(k):
        return (grp, hi * MERGE + (lo ^ k))

    def outer_peer(j):
        return (grp, (hi ^ j) * MERGE + lo)

    def group_peer(j):
        return (grp ^ j, me)

    peers = [inner_peer(k) for k in range(1, MERGE)]
    peers += [outer_peer(j) for j in range(1, outer)]
    peers += [group_peer(j) for j in range(1, groups)]
    barrier = pltpu.get_barrier_semaphore()
    for peer in peers:
        pl.semaphore_signal(barrier, inc=1, device_id=peer, device_id_type=pl.DeviceIdType.MESH)
    pl.semaphore_wait(barrier, len(peers))

    def remote(source, target, sems, index, peer):
        copy = pltpu.make_async_remote_copy(
            src_ref=source, dst_ref=target,
            send_sem=sems.at[(0,) + index], recv_sem=sems.at[(1,) + index],
            device_id=peer, device_id_type=pl.DeviceIdType.MESH,
        )
        copy.start()
        return copy

    def columns(j, k):
        owner = (hi ^ j) * MERGE + (lo ^ k)
        return pl.ds(pl.multiple_of(owner * rows, rows), rows)

    order = list(range(1, outer)) + [0]
    pending = []
    local = []
    got_w = []
    for i, weights in enumerate((ws_ref, wn_ref)):
        own = pltpu.make_async_copy(weights, wm.at[i, 0], l_sems.at[0, i])
        own.start()
        local.append(own)
        for k in range(1, MERGE):
            got_w.append(remote(weights, wm.at[i, k], w_sems, (i, k), inner_peer(k)))
    got = {}
    for j in order:
        got[j] = []
        for i, (whole, merged, sems) in enumerate(((x_ref, xm, x_sems), (a_ref, am, a_sems))):
            own = pltpu.make_async_copy(
                whole.at[:, columns(j, 0)], merged.at[j, 0], l_sems.at[1 + j, i])
            own.start()
            local.append(own)
            for k in range(1, MERGE):
                got[j].append(remote(
                    whole.at[:, columns(j, k)], merged.at[j, k], sems, (j, k), inner_peer(k)))
    for copy in local:
        copy.wait()
    for copy in got_w:
        copy.wait_recv()
    pending += got_w

    merged_cols = MERGE * fcols

    def partial_pre(j):
        for copy in got[j]:
            copy.wait_recv()
        pending.extend(got[j])
        total = lax.dot_general(
            xm[j].reshape(merged_cols, rows), wm[0].reshape(merged_cols, width),
            (((0,), (0,)), ((), ())), preferred_element_type=jnp.float32)
        return total + lax.dot_general(
            am[j].reshape(merged_cols, rows), wm[1].reshape(merged_cols, width),
            (((0,), (0,)), ((), ())), preferred_element_type=jnp.float32)

    sent = []
    for j in range(1, outer):
        psend[j] = partial_pre(j).astype(psend.dtype)
        sent.append(remote(psend.at[j], precv.at[j], p_sems, (j,), outer_peer(j)))
    pre = partial_pre(0) + bias_ref[...]
    for j in range(1, outer):
        sent[j - 1].wait_recv()
        pre = pre + precv[j].astype(jnp.float32)
    pending += sent
    square = pre * pre
    t = jnp.tanh(ROOT * pre * (1.0 + CUBIC * square))
    half = 0.5 * (1.0 + t)
    hidden_ref[...] = (pre * half).astype(hidden_ref.dtype)
    slope = half + 0.5 * pre * (1.0 - t * t) * (ROOT * (1.0 + 3.0 * CUBIC * square))
    dall[0] = (slope * up_ref[...].astype(jnp.float32)).astype(dall.dtype)
    sent = [remote(dall.at[0], dall.at[j], d_sems, (j,), outer_peer(j)) for j in range(1, outer)]

    colsum = jnp.zeros((1, width), jnp.float32)
    for j in range(outer):
        if j > 0:
            sent[j - 1].wait_recv()
        delta = dall[j]
        colsum = colsum + jnp.sum(delta.astype(jnp.float32), axis=0, keepdims=True)
        for i, merged in enumerate((xm, am)):
            part = jnp.dot(
                merged[j].reshape(merged_cols, rows), delta, preferred_element_type=jnp.float32
            ).reshape(MERGE, fcols, width)
            if j == 0:
                gacc[i] = part
            else:
                gacc[i] = gacc[i] + part
    pending += sent
    high = colsum.astype(jnp.bfloat16)
    low = (colsum - high.astype(jnp.float32)).astype(jnp.bfloat16)
    row_id = lax.broadcasted_iota(jnp.int32, (16, width), 0)
    tag = jnp.where(
        row_id == 0, high.astype(jnp.float32),
        jnp.where(row_id == 1, low.astype(jnp.float32), 0.0)).astype(jnp.bfloat16)
    sent = []
    for k in range(1, MERGE):
        gsend[k, 0:fcols] = gacc[0, k].astype(gsend.dtype)
        gsend[k, fcols:2 * fcols] = gacc[1, k].astype(gsend.dtype)
        gsend[k, 2 * fcols:2 * fcols + 16] = tag
        sent.append(remote(gsend.at[k], grecv.at[k], g_sems, (k,), inner_peer(k)))
    total_s = gacc[0, 0]
    total_n = gacc[1, 0]
    total_b = jnp.where(row_id == 0, colsum, 0.0)
    for k in range(1, MERGE):
        sent[k - 1].wait_recv()
        total_s = total_s + grecv[k, 0:fcols].astype(jnp.float32)
        total_n = total_n + grecv[k, fcols:2 * fcols].astype(jnp.float32)
        total_b = total_b + grecv[k, 2 * fcols:2 * fcols + 16].astype(jnp.float32)
    pending += sent
    vsend[0:fcols] = total_s
    vsend[fcols:2 * fcols] = total_n
    vsend[2 * fcols:2 * fcols + 16] = total_b
    sent = [remote(vsend, vrecv.at[j], v_sems, (j,), group_peer(j)) for j in range(1, groups)]
    for j in range(1, groups):
        sent[j - 1].wait_recv()
        total_s = total_s + vrecv[j, 0:fcols]
        total_n = total_n + vrecv[j, fcols:2 * fcols]
        total_b = total_b + vrecv[j, 2 * fcols:2 * fcols + 16]
    pending += sent
    gs_ref[...] = total_s
    gn_ref[...] = total_n
    gb_ref[...] = jnp.sum(total_b, axis=0, keepdims=True)
    for copy in pending:
        copy.wait_send()


def exchange(feats, aggregated, w_self, w_neigh, bias, upstream):
    groups = lax.axis_size("vgroup")
    nfeat = lax.axis_size("feat")
    outer = nfeat // MERGE
    fcols, width = w_self.shape
    rows = upstream.shape[0]
    any_spec = pl.BlockSpec(memory_space=pl.ANY)
    vmem_spec = pl.BlockSpec(memory_space=pltpu.VMEM)
    dma = pltpu.SemaphoreType.DMA
    return pl.pallas_call(
        functools.partial(exchange_kernel, groups, nfeat),
        out_shape=(
            jax.ShapeDtypeStruct((rows, width), jnp.bfloat16),
            jax.ShapeDtypeStruct((fcols, width), jnp.float32),
            jax.ShapeDtypeStruct((fcols, width), jnp.float32),
            jax.ShapeDtypeStruct((1, width), jnp.float32),
        ),
        in_specs=[any_spec] * 4 + [vmem_spec] * 2,
        out_specs=(vmem_spec,) * 4,
        scratch_shapes=[
            pltpu.VMEM((outer, MERGE, fcols, rows), jnp.bfloat16),
            pltpu.VMEM((outer, MERGE, fcols, rows), jnp.bfloat16),
            pltpu.VMEM((2, MERGE, fcols, width), jnp.bfloat16),
            pltpu.VMEM((outer, rows, width), jnp.bfloat16),
            pltpu.VMEM((outer, rows, width), jnp.bfloat16),
            pltpu.VMEM((outer, rows, width), jnp.bfloat16),
            pltpu.VMEM((2, MERGE, fcols, width), jnp.float32),
            pltpu.VMEM((MERGE, 2 * fcols + 16, width), jnp.bfloat16),
            pltpu.VMEM((MERGE, 2 * fcols + 16, width), jnp.bfloat16),
            pltpu.VMEM((2 * fcols + 16, width), jnp.float32),
            pltpu.VMEM((groups, 2 * fcols + 16, width), jnp.float32),
            dma((2, outer, MERGE)),
            dma((2, outer, MERGE)),
            dma((2, 2, MERGE)),
            dma((2, outer)),
            dma((2, outer)),
            dma((2, MERGE)),
            dma((2, groups)),
            dma((1 + outer, 2)),
        ],
        compiler_params=pltpu.CompilerParams(
            collective_id=0, has_side_effects=True, vmem_limit_bytes=40 * 2**20),
        name="exchange",
    )(feats, aggregated, w_self, w_neigh, bias.reshape(1, width), upstream)


def body(
    features_t, tile_weights, tile_dst, tile_src, tile_count, w_self, w_neigh, bias, grad_hidden
):
    feats = features_t[0]
    ndst = grad_hidden.shape[0] * lax.axis_size("feat")
    aggregated = aggregate(feats, tile_weights[0], tile_dst[0], tile_src[0], tile_count, ndst)
    hidden, grad_self, grad_neigh, grad_bias = exchange(
        feats, aggregated, w_self, w_neigh, bias, grad_hidden)
    return (hidden, grad_self, grad_neigh, grad_bias[0])


def solution(mesh):
    return jax.shard_map(
        body,
        mesh=mesh,
        in_specs=(
            P("vgroup", "feat", None),
            P("vgroup", None, None, None),
            P("vgroup", None),
            P("vgroup", None),
            P("vgroup"),
            P("feat", None),
            P("feat", None),
            P(),
            P(("vgroup", "feat"), None),
        ),
        out_specs=(P(("vgroup", "feat"), None), P("feat", None), P("feat", None), P()),
        check_vma=False,
    )
```

time: 295 us -> 95.9 us (0.33)
  waiting for transfers between devices: 158 us -> 0 us
  Pallas kernels: 0 us -> 88.9 us
  matrix products: 60.8 us -> 0 us
  blocking collectives: 39.3 us -> 0 us
  local copies, waits for them, and re-layouts: 20 us -> 5.49 us
  between operations: 14.5 us -> 1.37 us
    reduce_scatter x1 -> x0, waiting for transfers between devices: 107 us -> none  [body(): lax.psum_scatter(left_product(target_columns, w_self) + left_product(aggr...]
    pallas_call x0 -> x2, Pallas kernels: none -> 88.9 us  [the longest x1 67.7 us: exchange(): pl.pallas_call(functools.partial(exchange_kernel, groups, nfeat), out_sha...]
    dot_general x6 -> x0, matrix products: 60.8 us -> none  [the longest x1 25.4 us: body(): jnp.einsum('dt,ftj->fdj', onehot, product, precision=lax.Precision.HIGHEST)]
    all_gather x1 -> x0, waiting for transfers between devices: 50.4 us -> none  [gathered_grads(): piece = lax.all_gather(delta, 'feat', axis=0, tiled=True)]
    psum x1 -> x0, blocking collectives: 39.3 us -> none  [gathered_grads(): lax.psum(jnp.sum(delta, axis=0, dtype=jnp.float32), ('vgroup', 'feat'))]
    gather x1 -> x0, local copies, waits for them, and re-layouts: 13.5 us -> none  [body(): picked = jnp.take(source_blocks, srcs, axis=1)]
  transfers between devices with their start and end apart: 3 -> 0, of which waited for: 2 -> 0; matrix products, arithmetic and copies ran while one was open for 0% -> 0% of each run, Pallas kernels for 0% -> 0%
where the time goes in v1:
time: 95.9 us; the launch traced here: 95.7 us
  Pallas kernels  88.9 us (93%)
  local copies, waits for them, and re-layouts  5.49 us (6%)
  between operations  1.37 us (1%)
    pallas_call x1, Pallas kernels, exchange(): pl.pallas_call(functools.partial(exchange_kernel, groups, nfeat), out_sha...  67.7 us
    pallas_call x1, Pallas kernels, aggregate(): pl.pallas_call(aggregate_kernel, grid_spec=pltpu.PrefetchScalarGridSpec(n...  21.2 us
    unnamed x20, local copies, waits for them, and re-layouts  5.49 us

profile of v1, /device:TPU:0, one launch (start us, length us, event | category | flops | bytes accessed | tf_op | source)
XLA Modules:
  0.0 95.7 jit_solution(2204067414960526051)
XLA Ops:
  0.6 0.0 copy-start.7
  1.3 0.0 copy-start
  1.3 1.6 %copy-done = bf16[1,64,16384]{2,1,0:T(8,128)(2,1)S(1)} copy-done((bf16[1,64,16384]{2,1,0:T(8,128)(2,1)S(1)}, bf16[1,64,16384]{2,1,0:T(8,128)(2,1)}, u32[]{:S(2)}) %copy-start) | copy-done | bytes 2097176
  2.9 0.0 copy-start.5
  2.9 0.7 copy-done.5
  3.6 0.0 copy-start.6
  3.6 0.7 copy-done.6
  4.3 0.0 copy-start.1
  4.3 0.0 copy-start.2
  4.3 0.0 copy-start.3
  4.3 0.0 copy-start.4
  4.3 21.2 %aggregate.1.a_ref = bf16[64,8192]{1,0:T(8,128)(2,1)S(1)} custom-call(s32[512]{0:T(512)S(1)} %bitcast.8, s32[512]{0:T(512)S(1)} %bitcast.9, s32[1]{0:T(128)S(6)} %copy.17.count_ref, bf16[64,16384]{1,0:T(8,128)(2,1)S(1)} %bitcast.6, bf16[512,128,128]{2,1,0:T(8,128)(2,1)} %bitcast.12), custom_call_target="tpu_custom_call" | custom-call | flops 1073741824 | bytes 16777216 | tf_op jit(solution)/shard_map/aggregate/pallas_call | solution.py:45
  25.5 0.0 copy-done.7
  25.5 0.0 copy-done.1
  25.5 0.0 copy-done.2
  25.5 0.0 copy-done.3
  25.5 0.0 copy-done.4
  25.5 67.7 %exchange.1 = (bf16[512,256]{1,0:T(8,128)(2,1)S(1)}, f32[64,256]{1,0:T(8,128)S(1)}, f32[64,256]{1,0:T(8,128)S(1)}, f32[1,256]{1,0:T(1,128)S(1)}) custom-call(bf16[64,16384]{1,0:T(8,128)(2,1)S(1)} %bitcast.7, bf16[64,8192]{1,0:T(8,128)(2,1)S(1)} %aggregate.1.a_ref, bf16[64,256]{1,0:T(8,128)(2,1)S(1)} %copy-done.3, bf16[64,256]{1,0:T(8,128)(2,1)S(1)} %copy-done.4, ...), custom_call_target="tpu_custom_call" | custom-call | tf_op jit(solution)/shard_map/exchange/pallas_call | solution.py:237
  93.2 0.7 copy.18
  93.9 0.6 copy.19
  94.5 0.6 copy.20
  95.2 0.6 copy.21
Async XLA Ops:
  0.6 24.8 %copy-start.7 = (f32[256]{0:T(256)S(1)}, f32[256]{0:T(256)}, u32[]{:S(2)}) copy-start(f32[256]{0:T(256)} %param.16) | copy-start | bytes 3076
  1.3 1.6 %copy-start = (bf16[1,64,16384]{2,1,0:T(8,128)(2,1)S(1)}, bf16[1,64,16384]{2,1,0:T(8,128)(2,1)}, u32[]{:S(2)}) copy-start(bf16[1,64,16384]{2,1,0:T(8,128)(2,1)} %param.9) | copy-start | bytes 6291460
  2.9 0.7 copy-start.5
  3.6 0.7 copy-start.6
  4.3 21.2 %copy-start.1 = (bf16[1,64,16384]{2,1,0:T(8,128)(2,1)S(1)}, bf16[1,64,16384]{2,1,0:T(8,128)(2,1)}, u32[]{:S(2)}) copy-start(bf16[1,64,16384]{2,1,0:T(8,128)(2,1)} %param.9) | copy-start | bytes 6291460
  4.3 21.2 %copy-start.2 = (bf16[512,256]{1,0:T(8,128)(2,1)S(1)}, bf16[512,256]{1,0:T(8,128)(2,1)}, u32[]{:S(2)}) copy-start(bf16[512,256]{1,0:T(8,128)(2,1)} %up_ref.1) | copy-start | bytes 786436
  4.3 21.2 %copy-start.3 = (bf16[64,256]{1,0:T(8,128)(2,1)S(1)}, bf16[64,256]{1,0:T(8,128)(2,1)}, u32[]{:S(2)}) copy-start(bf16[64,256]{1,0:T(8,128)(2,1)} %ws_ref.1) | copy-start | bytes 98308
  4.3 21.2 %copy-start.4 = (bf16[64,256]{1,0:T(8,128)(2,1)S(1)}, bf16[64,256]{1,0:T(8,128)(2,1)}, u32[]{:S(2)}) copy-start(bf16[64,256]{1,0:T(8,128)(2,1)} %wn_ref.1) | copy-start | bytes 98308

commit v2 on v1

--- a/solution.py
+++ b/solution.py
@@ -8,35 +8,50 @@
 from jax.sharding import PartitionSpec as P
 
 STEP = 64
-UNROLL = 8
-
-
-def aggregate_kernel(dst_ref, src_ref, count_ref, x_ref, w_ref, out_ref, acc_ref):
+HALF = 16
+
+
+def aggregate_kernel(dst_ref, src_ref, count_ref, x_ref, w_ref, out_ref, acc_a, acc_b, buf_a, buf_b):
     step = pl.program_id(0)
     tile = w_ref.shape[1]
     dtiles = out_ref.shape[1] // tile
+    base = step * STEP
 
     @pl.when(step == 0)
     def _():
-        acc_ref[...] = jnp.zeros_like(acc_ref)
-
-    @pl.loop(0, STEP // UNROLL)
-    def _(group):
-        for k in range(UNROLL):
-            i = group * UNROLL + k
-            t = step * STEP + i
-            d = jnp.where(t < count_ref[0], dst_ref[t], dtiles)
-            s = pl.multiple_of(src_ref[t] * tile, tile)
-            prod = lax.dot_general(
-                x_ref[:, pl.ds(s, tile)], w_ref[i], (((1,), (1,)), ((), ())),
+        acc_a[...] = jnp.zeros_like(acc_a)
+        acc_b[...] = jnp.zeros_like(acc_b)
+        buf_b[...] = jnp.zeros_like(buf_b)
+
+    def multiply(first, buf):
+        for k in range(HALF):
+            s = pl.multiple_of(src_ref[base + first + k] * tile, tile)
+            buf[k] = lax.dot_general(
+                x_ref[:, pl.ds(s, tile)], w_ref[first + k], (((1,), (1,)), ((), ())),
                 preferred_element_type=jnp.float32,
             )
-            acc_ref[d] = acc_ref[d] + prod
+
+    def add(first, buf):
+        for k in range(HALF):
+            t = first + k
+            live = jnp.logical_and(t >= 0, t < count_ref[0])
+            d = jnp.where(live, dst_ref[jnp.maximum(t, 0)], dtiles)
+            acc = (acc_a, acc_b)[k % 2]
+            acc[d] = acc[d] + buf[k]
+
+    @pl.loop(0, STEP // (2 * HALF))
+    def _(pair):
+        first = pair * 2 * HALF
+        multiply(first, buf_a)
+        add(base + first - HALF, buf_b)
+        multiply(first + HALF, buf_b)
+        add(base + first, buf_a)
 
     @pl.when(step == pl.num_programs(0) - 1)
     def _():
+        add(base + STEP - HALF, buf_b)
         for d in range(dtiles):
-            out_ref[:, d * tile:(d + 1) * tile] = acc_ref[d].astype(out_ref.dtype)
+            out_ref[:, d * tile:(d + 1) * tile] = (acc_a[d] + acc_b[d]).astype(out_ref.dtype)
 
 
 def aggregate(feats, tiles, dsts, srcs, count, ndst):
@@ -52,7 +67,8 @@
                 pl.BlockSpec((STEP, tile, tile), lambda i, *_: (i, 0, 0)),
             ],
             out_specs=pl.BlockSpec((fcols, ndst), lambda i, *_: (0, 0), pipeline_mode=pl.Buffered(1)),
-            scratch_shapes=[pltpu.VMEM((ndst // tile + 1, fcols, tile), jnp.float32)],
+            scratch_shapes=[pltpu.VMEM((ndst // tile + 1, fcols, tile), jnp.float32)] * 2
+            + [pltpu.VMEM((HALF, fcols, tile), jnp.float32)] * 2,
         ),
         out_shape=jax.ShapeDtypeStruct((fcols, ndst), jnp.bfloat16),
         compiler_params=pltpu.CompilerParams(vmem_limit_bytes=40 * 2**20),
@@ -124,7 +140,8 @@
         own.start()
         local.append(own)
         for k in range(1, MERGE):
-            got_w.append(remote(weights, wm.at[i, k], w_sems, (i, k), inner_peer(k)))
+            if k == 1 or k % 2 == 0:
+                got_w.append(remote(weights, wm.at[i, k], w_sems, (i, k), inner_peer(k)))
     got = {}
     for j in order:
         got[j] = []
@@ -138,6 +155,13 @@
                     whole.at[:, columns(j, k)], merged.at[j, k], sems, (j, k), inner_peer(k)))
     for copy in local:
         copy.wait()
+    for copy in got_w:
+        copy.wait_recv()
+    pending += got_w
+    got_w = [
+        remote(wm.at[i, k - 1], wm.at[i, k], w_sems, (i, k), inner_peer(1))
+        for i in range(2) for k in range(3, MERGE, 2)
+    ]
     for copy in got_w:
         copy.wait_recv()
     pending += got_w

time: 95.9 us -> 88.5 us (0.923)
  Pallas kernels: 88.9 us -> 81.5 us
    pallas_call x1, Pallas kernels: 21.2 us -> 16.4 us  [aggregate(): pl.pallas_call(aggregate_kernel, grid_spec=pltpu.PrefetchScalarGridSpec(n...]
    pallas_call x1, Pallas kernels: 67.7 us -> 65.1 us  [exchange(): pl.pallas_call(functools.partial(exchange_kernel, groups, nfeat), out_sha...]
where the time goes in v2:
time: 88.5 us; the launch traced here: 88.4 us
  Pallas kernels  81.5 us (92%)
  local copies, waits for them, and re-layouts  5.49 us (6%)
  between operations  1.37 us (2%)
    pallas_call x1, Pallas kernels, exchange(): pl.pallas_call(functools.partial(exchange_kernel, groups, nfeat), out_sha...  65.1 us
    pallas_call x1, Pallas kernels, aggregate(): pl.pallas_call(aggregate_kernel, grid_spec=pltpu.PrefetchScalarGridSpec(n...  16.4 us
    unnamed x20, local copies, waits for them, and re-layouts  5.49 us

profile of v2, /device:TPU:0, one launch (start us, length us, event | category | flops | bytes accessed | tf_op | source)
XLA Modules:
  0.0 88.4 jit_solution(11958811965947258163)
XLA Ops:
  0.6 0.0 copy-start.7
  1.3 0.0 copy-start
  1.3 1.6 %copy-done = bf16[1,64,16384]{2,1,0:T(8,128)(2,1)S(1)} copy-done((bf16[1,64,16384]{2,1,0:T(8,128)(2,1)S(1)}, bf16[1,64,16384]{2,1,0:T(8,128)(2,1)}, u32[]{:S(2)}) %copy-start) | copy-done | bytes 2097176
  2.9 0.0 copy-start.5
  2.9 0.7 copy-done.5
  3.6 0.0 copy-start.6
  3.6 0.7 copy-done.6
  4.3 0.0 copy-start.1
  4.3 0.0 copy-start.2
  4.3 0.0 copy-start.3
  4.3 0.0 copy-start.4
  4.3 16.4 %aggregate.1.a_ref = bf16[64,8192]{1,0:T(8,128)(2,1)S(1)} custom-call(s32[512]{0:T(512)S(1)} %bitcast.8, s32[512]{0:T(512)S(1)} %bitcast.9, s32[1]{0:T(128)S(6)} %copy.17.count_ref, bf16[64,16384]{1,0:T(8,128)(2,1)S(1)} %bitcast.6, bf16[512,128,128]{2,1,0:T(8,128)(2,1)} %bitcast.12), custom_call_target="tpu_custom_call" | custom-call | flops 1073741824 | bytes 16777216 | tf_op jit(solution)/shard_map/aggregate/pallas_call | solution.py:60
  20.7 0.0 copy-done.7
  20.7 0.0 copy-done.1
  20.7 0.0 copy-done.2
  20.7 0.0 copy-done.3
  20.7 0.0 copy-done.4
  20.8 65.1 %exchange.1 = (bf16[512,256]{1,0:T(8,128)(2,1)S(1)}, f32[64,256]{1,0:T(8,128)S(1)}, f32[64,256]{1,0:T(8,128)S(1)}, f32[1,256]{1,0:T(1,128)S(1)}) custom-call(bf16[64,16384]{1,0:T(8,128)(2,1)S(1)} %bitcast.7, bf16[64,8192]{1,0:T(8,128)(2,1)S(1)} %aggregate.1.a_ref, bf16[64,256]{1,0:T(8,128)(2,1)S(1)} %copy-done.3, bf16[64,256]{1,0:T(8,128)(2,1)S(1)} %copy-done.4, ...), custom_call_target="tpu_custom_call" | custom-call | tf_op jit(solution)/shard_map/exchange/pallas_call | solution.py:261
  85.8 0.7 copy.18
  86.5 0.6 copy.19
  87.2 0.6 copy.20
  87.8 0.6 copy.21
Async XLA Ops:
  0.6 20.1 %copy-start.7 = (f32[256]{0:T(256)S(1)}, f32[256]{0:T(256)}, u32[]{:S(2)}) copy-start(f32[256]{0:T(256)} %param.16) | copy-start | bytes 3076
  1.3 1.6 %copy-start = (bf16[1,64,16384]{2,1,0:T(8,128)(2,1)S(1)}, bf16[1,64,16384]{2,1,0:T(8,128)(2,1)}, u32[]{:S(2)}) copy-start(bf16[1,64,16384]{2,1,0:T(8,128)(2,1)} %param.9) | copy-start | bytes 6291460
  2.9 0.7 copy-start.5
  3.6 0.7 copy-start.6
  4.3 16.5 %copy-start.1 = (bf16[1,64,16384]{2,1,0:T(8,128)(2,1)S(1)}, bf16[1,64,16384]{2,1,0:T(8,128)(2,1)}, u32[]{:S(2)}) copy-start(bf16[1,64,16384]{2,1,0:T(8,128)(2,1)} %param.9) | copy-start | bytes 6291460
  4.3 16.5 %copy-start.2 = (bf16[512,256]{1,0:T(8,128)(2,1)S(1)}, bf16[512,256]{1,0:T(8,128)(2,1)}, u32[]{:S(2)}) copy-start(bf16[512,256]{1,0:T(8,128)(2,1)} %up_ref.1) | copy-start | bytes 786436
  4.3 16.5 %copy-start.3 = (bf16[64,256]{1,0:T(8,128)(2,1)S(1)}, bf16[64,256]{1,0:T(8,128)(2,1)}, u32[]{:S(2)}) copy-start(bf16[64,256]{1,0:T(8,128)(2,1)} %ws_ref.1) | copy-start | bytes 98308
  4.3 16.5 %copy-start.4 = (bf16[64,256]{1,0:T(8,128)(2,1)S(1)}, bf16[64,256]{1,0:T(8,128)(2,1)}, u32[]{:S(2)}) copy-start(bf16[64,256]{1,0:T(8,128)(2,1)} %wn_ref.1) | copy-start | bytes 98308

commit v3 on v2

--- a/solution.py
+++ b/solution.py
@@ -85,15 +85,59 @@
 ROOT = 0.7978845608
 
 
+def arrange_kernel(outer, x_ref, ws_ref, wn_ref, *refs):
+    outs, sems = refs[:MERGE // 2], refs[MERGE // 2]
+    fcols, width = ws_ref.shape
+    rows = outs[0].shape[1]
+    me = lax.axis_index("feat")
+    copies = []
+    for p, out in enumerate(outs):
+        for side in range(2):
+            for j in range(outer):
+                owner = me ^ (j * MERGE + 2 * p + side)
+                columns = pl.ds(pl.multiple_of(owner * rows, rows), rows)
+                place = side * outer + j
+                copies.append(pltpu.make_async_copy(
+                    x_ref.at[:, columns], out.at[pl.ds(place * fcols, fcols)], sems.at[p, place]))
+        for i, weights in enumerate((ws_ref, wn_ref)):
+            copies.append(pltpu.make_async_copy(
+                weights, out.at[pl.ds(2 * outer * fcols, fcols), pl.ds(i * width, width)],
+                sems.at[p, 2 * outer + i]))
+    for copy in copies:
+        copy.start()
+    for copy in copies:
+        copy.wait()
+
+
+def arrange(feats, w_self, w_neigh, rows):
+    outer = lax.axis_size("feat") // MERGE
+    fcols, width = w_self.shape
+    any_spec = pl.BlockSpec(memory_space=pl.ANY)
+    pieces = pl.pallas_call(
+        functools.partial(arrange_kernel, outer),
+        out_shape=(jax.ShapeDtypeStruct(((2 * outer + 1) * fcols, rows), jnp.bfloat16),) * (MERGE // 2),
+        in_specs=[any_spec] * 3,
+        out_specs=(any_spec,) * (MERGE // 2),
+        scratch_shapes=[pltpu.SemaphoreType.DMA((MERGE // 2, 2 * outer + 2))],
+        name="arrange",
+    )(feats, w_self, w_neigh)
+    nfeat = lax.axis_size("feat")
+    moved = [pieces[0]]
+    for p in range(1, MERGE // 2):
+        moved.append(lax.ppermute(pieces[p], "feat", [(f, f ^ (2 * p)) for f in range(nfeat)]))
+    return moved
+
+
 def exchange_kernel(
     groups, nfeat,
-    x_ref, a_ref, ws_ref, wn_ref, bias_ref, up_ref,
-    hidden_ref, gs_ref, gn_ref, gb_ref,
-    xm, am, wm, psend, precv, dall, gacc, gsend, grecv, vsend, vrecv,
-    x_sems, a_sems, w_sems, p_sems, d_sems, g_sems, v_sems, l_sems,
+    *refs,
 ):
+    moved, refs = refs[:MERGE // 2], refs[MERGE // 2:]
+    a_ref, bias_ref, up_ref, hidden_ref, gs_ref, gn_ref, gb_ref, *refs = refs
+    xm, am, wm, psend, precv, dall, gacc, gsend, grecv, vsend, vrecv, *refs = refs
+    a_sems, s_sems, p_sems, d_sems, g_sems, v_sems, l_sems, own_sems = refs
     outer = nfeat // MERGE
-    fcols = ws_ref.shape[0]
+    fcols = a_ref.shape[0]
     rows = up_ref.shape[0]
     width = up_ref.shape[1]
     grp = lax.axis_index("vgroup")
@@ -134,47 +178,44 @@
     order = list(range(1, outer)) + [0]
     pending = []
     local = []
-    got_w = []
-    for i, weights in enumerate((ws_ref, wn_ref)):
-        own = pltpu.make_async_copy(weights, wm.at[i, 0], l_sems.at[0, i])
-        own.start()
-        local.append(own)
-        for k in range(1, MERGE):
-            if k == 1 or k % 2 == 0:
-                got_w.append(remote(weights, wm.at[i, k], w_sems, (i, k), inner_peer(k)))
     got = {}
     for j in order:
-        got[j] = []
-        for i, (whole, merged, sems) in enumerate(((x_ref, xm, x_sems), (a_ref, am, a_sems))):
-            own = pltpu.make_async_copy(
-                whole.at[:, columns(j, 0)], merged.at[j, 0], l_sems.at[1 + j, i])
-            own.start()
-            local.append(own)
-            for k in range(1, MERGE):
-                got[j].append(remote(
-                    whole.at[:, columns(j, k)], merged.at[j, k], sems, (j, k), inner_peer(k)))
+        got[j] = [
+            remote(a_ref.at[:, columns(j, k)], am.at[j, k], a_sems, (j, k), inner_peer(k))
+            for k in range(1, MERGE)
+        ]
+    for j in order:
+        local.append(pltpu.make_async_copy(a_ref.at[:, columns(j, 0)], am.at[j, 0], own_sems.at[j]))
+    shared = []
+    for p, piece in enumerate(moved):
+        k = 2 * p
+        for j in range(outer):
+            local.append(pltpu.make_async_copy(
+                piece.at[pl.ds(j * fcols, fcols)], xm.at[j, k], l_sems.at[p, j]))
+            shared.append(remote(
+                piece.at[pl.ds((outer + j) * fcols, fcols)], xm.at[j, k + 1],
+                s_sems, (p, j), inner_peer(1)))
+        for i in range(2):
+            weights = piece.at[pl.ds(2 * outer * fcols, fcols), pl.ds(i * width, width)]
+            local.append(pltpu.make_async_copy(weights, wm.at[i, k], l_sems.at[p, outer + i]))
+            shared.append(remote(weights, wm.at[i, k + 1], s_sems, (p, outer + i), inner_peer(1)))
+    for copy in local:
+        copy.start()
     for copy in local:
         copy.wait()
-    for copy in got_w:
+    for copy in shared:
         copy.wait_recv()
-    pending += got_w
-    got_w = [
-        remote(wm.at[i, k - 1], wm.at[i, k], w_sems, (i, k), inner_peer(1))
-        for i in range(2) for k in range(3, MERGE, 2)
-    ]
-    for copy in got_w:
-        copy.wait_recv()
-    pending += got_w
+    pending += shared
 
     merged_cols = MERGE * fcols
 
     def partial_pre(j):
+        total = lax.dot_general(
+            xm[j].reshape(merged_cols, rows), wm[0].reshape(merged_cols, width),
+            (((0,), (0,)), ((), ())), preferred_element_type=jnp.float32)
         for copy in got[j]:
             copy.wait_recv()
         pending.extend(got[j])
-        total = lax.dot_general(
-            xm[j].reshape(merged_cols, rows), wm[0].reshape(merged_cols, width),
-            (((0,), (0,)), ((), ())), preferred_element_type=jnp.float32)
         return total + lax.dot_general(
             am[j].reshape(merged_cols, rows), wm[1].reshape(merged_cols, width),
             (((0,), (0,)), ((), ())), preferred_element_type=jnp.float32)
@@ -249,12 +290,12 @@
         copy.wait_send()
 
 
-def exchange(feats, aggregated, w_self, w_neigh, bias, upstream):
+def exchange(moved, aggregated, bias, upstream):
     groups = lax.axis_size("vgroup")
     nfeat = lax.axis_size("feat")
     outer = nfeat // MERGE
-    fcols, width = w_self.shape
-    rows = upstream.shape[0]
+    fcols = aggregated.shape[0]
+    rows, width = upstream.shape
     any_spec = pl.BlockSpec(memory_space=pl.ANY)
     vmem_spec = pl.BlockSpec(memory_space=pltpu.VMEM)
     dma = pltpu.SemaphoreType.DMA
@@ -266,7 +307,7 @@
             jax.ShapeDtypeStruct((fcols, width), jnp.float32),
             jax.ShapeDtypeStruct((1, width), jnp.float32),
         ),
-        in_specs=[any_spec] * 4 + [vmem_spec] * 2,
+        in_specs=[any_spec] * (MERGE // 2 + 1) + [vmem_spec] * 2,
         out_specs=(vmem_spec,) * 4,
         scratch_shapes=[
             pltpu.VMEM((outer, MERGE, fcols, rows), jnp.bfloat16),
@@ -281,18 +322,18 @@
             pltpu.VMEM((2 * fcols + 16, width), jnp.float32),
             pltpu.VMEM((groups, 2 * fcols + 16, width), jnp.float32),
             dma((2, outer, MERGE)),
-            dma((2, outer, MERGE)),
-            dma((2, 2, MERGE)),
+            dma((2, MERGE // 2, outer + 2)),
             dma((2, outer)),
             dma((2, outer)),
             dma((2, MERGE)),
             dma((2, groups)),
-            dma((1 + outer, 2)),
+            dma((MERGE // 2, outer + 2)),
+            dma((outer,)),
         ],
         compiler_params=pltpu.CompilerParams(
             collective_id=0, has_side_effects=True, vmem_limit_bytes=40 * 2**20),
         name="exchange",
-    )(feats, aggregated, w_self, w_neigh, bias.reshape(1, width), upstream)
+    )(*moved, aggregated, bias.reshape(1, width), upstream)
 
 
 def body(
@@ -300,9 +341,9 @@
 ):
     feats = features_t[0]
     ndst = grad_hidden.shape[0] * lax.axis_size("feat")
+    moved = arrange(feats, w_self, w_neigh, grad_hidden.shape[0])
     aggregated = aggregate(feats, tile_weights[0], tile_dst[0], tile_src[0], tile_count, ndst)
-    hidden, grad_self, grad_neigh, grad_bias = exchange(
-        feats, aggregated, w_self, w_neigh, bias, grad_hidden)
+    hidden, grad_self, grad_neigh, grad_bias = exchange(moved, aggregated, bias, grad_hidden)
     return (hidden, grad_self, grad_neigh, grad_bias[0])
 
 

time: 88.5 us -> 122 us (1.38)
  Pallas kernels: 81.5 us -> 110 us
  starting transfers between devices: 0 us -> 4.61 us
    pallas_call x0 -> x1, Pallas kernels: none -> 41 us  [arrange(): pl.pallas_call(functools.partial(arrange_kernel, outer), out_shape=(jax.S...]
    pallas_call x1, Pallas kernels: 65.1 us -> 52.6 us  [exchange(): pl.pallas_call(functools.partial(exchange_kernel, groups, nfeat), out_sha...]
    ppermute x0 -> x3, starting transfers between devices: none -> 4.61 us  [arrange(): lax.ppermute(pieces[p], 'feat', [(f, f ^ 2 * p) for f in range(nfeat)])]
    unnamed x20 -> x16, local copies, waits for them, and re-layouts: 5.49 us -> 5.49 us
  transfers between devices with their start and end apart: 0 -> 3, of which waited for: 0 -> 0; matrix products, arithmetic and copies ran while one was open for 0% -> 0% of each run, Pallas kernels for 0% -> 13%
where the time goes in v3:
time: 122 us; the launch traced here: 121 us
  Pallas kernels  110 us (90%)
  local copies, waits for them, and re-layouts  5.49 us (4%)
  starting transfers between devices  4.61 us (4%)
  between operations  1.38 us (1%)
    pallas_call x1, Pallas kernels, exchange(): pl.pallas_call(functools.partial(exchange_kernel, groups, nfeat), out_sha...  52.6 us
    pallas_call x1, Pallas kernels, arrange(): pl.pallas_call(functools.partial(arrange_kernel, outer), out_shape=(jax.S...  41 us
    pallas_call x1, Pallas kernels, aggregate(): pl.pallas_call(aggregate_kernel, grid_spec=pltpu.PrefetchScalarGridSpec(n...  16.3 us
    unnamed x16, local copies, waits for them, and re-layouts  5.49 us
    ppermute x3, starting transfers between devices, arrange(): lax.ppermute(pieces[p], 'feat', [(f, f ^ 2 * p) for f in range(nfeat)])  4.61 us
  transfers between devices with their start and end apart: 3, of which 0 were waited for; matrix products, arithmetic and copies ran while one was open for 0% of the time, Pallas kernels for 13%

profile of v3, /device:TPU:0, one launch (start us, length us, event | category | flops | bytes accessed | tf_op | source)
XLA Modules:
  0.0 121.4 jit_solution(16576525440000256958)
XLA Ops:
  0.6 0.0 copy-start.2
  0.6 0.0 copy-start.5
  0.7 41.0 %arrange.1 = (bf16[320,512]{1,0:T(8,128)(2,1)}, bf16[320,512]{1,0:T(8,128)(2,1)}, bf16[320,512]{1,0:T(8,128)(2,1)}, bf16[320,512]{1,0:T(8,128)(2,1)}) custom-call(bf16[64,16384]{1,0:T(8,128)(2,1)} %bitcast.6, bf16[64,256]{1,0:T(8,128)(2,1)} %ws_ref.1, bf16[64,256]{1,0:T(8,128)(2,1)} %wn_ref.1), custom_call_target="tpu_custom_call" | custom-call | tf_op jit(solution)/shard_map/arrange/pallas_call | solution.py:116
  41.7 3.0 %collective-permute-start = (bf16[320,512]{1,0:T(8,128)(2,1)}, bf16[320,512]{1,0:T(8,128)(2,1)S(1)}, u32[]{:S(2)}, u32[]{:S(2)}) collective-permute-start(bf16[320,512]{1,0:T(8,128)(2,1)} %get-tuple-element.13), channel_id=1, source_target_pairs={{0,2},{1,3},{2,0},{3,1},{4,6},{5,7},{6,4},{7,5},{8,10},{9,11},{10,... | collective-permute-start | bytes 983048 | tf_op jit(solution)/shard_map/ppermute | solution.py:127
  44.7 1.6 %collective-permute-start.1 = (bf16[320,512]{1,0:T(8,128)(2,1)}, bf16[320,512]{1,0:T(8,128)(2,1)S(1)}, u32[]{:S(2)}, u32[]{:S(2)}) collective-permute-start(bf16[320,512]{1,0:T(8,128)(2,1)} %get-tuple-element.14), channel_id=1, source_target_pairs={{0,4},{1,5},{2,6},{3,7},{4,0},{5,1},{6,2},{7,3},{8,12},{9,13},{10,... | collective-permute-start | bytes 983048 | tf_op jit(solution)/shard_map/ppermute | solution.py:127
  46.3 0.0 collective-permute-start.2
  47.0 0.0 copy-start
  47.0 1.6 %copy-done = bf16[1,64,16384]{2,1,0:T(8,128)(2,1)S(1)} copy-done((bf16[1,64,16384]{2,1,0:T(8,128)(2,1)S(1)}, bf16[1,64,16384]{2,1,0:T(8,128)(2,1)}, u32[]{:S(2)}) %copy-start) | copy-done | bytes 2097176
  48.5 0.0 copy-start.3
  48.5 0.7 copy-done.3
  49.2 0.0 copy-start.4
  49.2 0.7 copy-done.4
  49.9 16.3 %aggregate.1.refs_4_ = bf16[64,8192]{1,0:T(8,128)(2,1)S(1)} custom-call(s32[512]{0:T(512)S(1)} %bitcast.8, s32[512]{0:T(512)S(1)} %bitcast.9, s32[1]{0:T(128)S(6)} %copy.17.count_ref, bf16[64,16384]{1,0:T(8,128)(2,1)S(1)} %bitcast.7, bf16[512,128,128]{2,1,0:T(8,128)(2,1)} %bitcast.12), custom_call_target="tpu_custom_call" | custom-call | flops 1073741824 | bytes 16777216 | tf_op jit(solution)/shard_map/aggregate/pallas_call | solution.py:60
  66.2 0.0 collective-permute-done.refs_1_
  66.2 0.0 collective-permute-done.1.refs_2_
  66.3 0.0 collective-permute-done.2.refs_3_
  66.3 0.0 copy-done.2
  66.3 0.0 copy-done.5
  66.3 0.0 copy-done.1
  66.3 52.6 %exchange.1 = (bf16[512,256]{1,0:T(8,128)(2,1)S(1)}, f32[64,256]{1,0:T(8,128)S(1)}, f32[64,256]{1,0:T(8,128)S(1)}, f32[1,256]{1,0:T(1,128)S(1)}) custom-call(bf16[320,512]{1,0:T(8,128)(2,1)S(1)} %copy-done.1, bf16[320,512]{1,0:T(8,128)(2,1)S(1)} %collective-permute-done.refs_1_, bf16[320,512]{1,0:T(8,128)(2,1)S(1)} %collective-permute-done.1.refs_2_, ...), custom_call_target="tpu_custom_call" | custom-call | tf_op jit(solution)/shard_map/exchange/pallas_call | solution.py:302
  118.9 0.7 copy.18
  119.6 0.6 copy.19
  120.2 0.6 copy.20
  120.9 0.6 copy.21
  (1 shorter events, 0.0 us)
Async XLA Ops:
  0.6 65.6 %copy-start.2 = (bf16[512,256]{1,0:T(8,128)(2,1)S(1)}, bf16[512,256]{1,0:T(8,128)(2,1)}, u32[]{:S(2)}) copy-start(bf16[512,256]{1,0:T(8,128)(2,1)} %refs_6_.1) | copy-start | bytes 786436
  0.6 65.6 %copy-start.5 = (f32[256]{0:T(256)S(1)}, f32[256]{0:T(256)}, u32[]{:S(2)}) copy-start(f32[256]{0:T(256)} %param.16) | copy-start | bytes 3076
  41.7 24.5 %collective-permute-start = (bf16[320,512]{1,0:T(8,128)(2,1)}, bf16[320,512]{1,0:T(8,128)(2,1)S(1)}, u32[]{:S(2)}, u32[]{:S(2)}) collective-permute-start(bf16[320,512]{1,0:T(8,128)(2,1)} %get-tuple-element.13), channel_id=1, source_target_pairs={{0,2},{1,3},{2,0},{3,1},{4,6},{5,7},{6,4},{7,5},{8,10},{9,11},{10,... | collective-permute-start | bytes 983048 | tf_op jit(solution)/shard_map/ppermute | solution.py:127
  44.7 21.5 %collective-permute-start.1 = (bf16[320,512]{1,0:T(8,128)(2,1)}, bf16[320,512]{1,0:T(8,128)(2,1)S(1)}, u32[]{:S(2)}, u32[]{:S(2)}) collective-permute-start(bf16[320,512]{1,0:T(8,128)(2,1)} %get-tuple-element.14), channel_id=1, source_target_pairs={{0,4},{1,5},{2,6},{3,7},{4,0},{5,1},{6,2},{7,3},{8,12},{9,13},{10,... | collective-permute-start | bytes 983048 | tf_op jit(solution)/shard_map/ppermute | solution.py:127
  46.3 20.0 %collective-permute-start.2 = (bf16[320,512]{1,0:T(8,128)(2,1)}, bf16[320,512]{1,0:T(8,128)(2,1)S(1)}, u32[]{:S(2)}, u32[]{:S(2)}) collective-permute-start(bf16[320,512]{1,0:T(8,128)(2,1)} %get-tuple-element.15), channel_id=1, source_target_pairs={{0,6},{1,7},{2,4},{3,5},{4,2},{5,3},{6,0},{7,1},{8,14},{9,15},{10,... | collective-permute-start | bytes 983048 | tf_op jit(solution)/shard_map/ppermute | solution.py:127
  47.0 1.6 %copy-start = (bf16[1,64,16384]{2,1,0:T(8,128)(2,1)S(1)}, bf16[1,64,16384]{2,1,0:T(8,128)(2,1)}, u32[]{:S(2)}) copy-start(bf16[1,64,16384]{2,1,0:T(8,128)(2,1)} %param.9) | copy-start | bytes 6291460
  48.5 0.7 copy-start.3
  49.2 0.7 copy-start.4
  49.9 16.4 %copy-start.1 = (bf16[320,512]{1,0:T(8,128)(2,1)S(1)}, bf16[320,512]{1,0:T(8,128)(2,1)}, u32[]{:S(2)}) copy-start(bf16[320,512]{1,0:T(8,128)(2,1)} %get-tuple-element.12.refs_0_) | copy-start | bytes 983044

commit v4 on v3

--- a/solution.py
+++ b/solution.py
@@ -24,12 +24,19 @@
         buf_b[...] = jnp.zeros_like(buf_b)
 
     def multiply(first, buf):
-        for k in range(HALF):
-            s = pl.multiple_of(src_ref[base + first + k] * tile, tile)
-            buf[k] = lax.dot_general(
-                x_ref[:, pl.ds(s, tile)], w_ref[first + k], (((1,), (1,)), ((), ())),
-                preferred_element_type=jnp.float32,
-            )
+        for k in range(0, HALF, 2):
+            one, two = [
+                x_ref[:, pl.ds(pl.multiple_of(src_ref[base + first + k + n] * tile, tile), tile)]
+                for n in range(2)
+            ]
+            zero = jnp.zeros_like(one)
+            left = jnp.concatenate([
+                jnp.concatenate([one, zero], axis=1), jnp.concatenate([zero, two], axis=1)], axis=0)
+            right = jnp.concatenate([w_ref[first + k], w_ref[first + k + 1]], axis=1)
+            prod = lax.dot_general(
+                left, right, (((1,), (1,)), ((), ())), preferred_element_type=jnp.float32)
+            buf[k] = prod[:one.shape[0]]
+            buf[k + 1] = prod[one.shape[0]:]
 
     def add(first, buf):
         for k in range(HALF):
@@ -81,47 +88,45 @@
 
 
 MERGE = 8
+PARTS = 2
 CUBIC = 0.044715
 ROOT = 0.7978845608
 
 
 def arrange_kernel(outer, x_ref, ws_ref, wn_ref, *refs):
-    outs, sems = refs[:MERGE // 2], refs[MERGE // 2]
+    outs = refs
     fcols, width = ws_ref.shape
     rows = outs[0].shape[1]
     me = lax.axis_index("feat")
-    copies = []
     for p, out in enumerate(outs):
         for side in range(2):
             for j in range(outer):
                 owner = me ^ (j * MERGE + 2 * p + side)
                 columns = pl.ds(pl.multiple_of(owner * rows, rows), rows)
                 place = side * outer + j
-                copies.append(pltpu.make_async_copy(
-                    x_ref.at[:, columns], out.at[pl.ds(place * fcols, fcols)], sems.at[p, place]))
-        for i, weights in enumerate((ws_ref, wn_ref)):
-            copies.append(pltpu.make_async_copy(
-                weights, out.at[pl.ds(2 * outer * fcols, fcols), pl.ds(i * width, width)],
-                sems.at[p, 2 * outer + i]))
-    for copy in copies:
-        copy.start()
-    for copy in copies:
-        copy.wait()
+                out[place * fcols:(place + 1) * fcols] = x_ref[:, columns]
+        last = slice(2 * outer * fcols, (2 * outer + 1) * fcols)
+        out[last, 0:width] = ws_ref[...]
+        out[last, width:2 * width] = wn_ref[...]
 
 
 def arrange(feats, w_self, w_neigh, rows):
     outer = lax.axis_size("feat") // MERGE
     fcols, width = w_self.shape
-    any_spec = pl.BlockSpec(memory_space=pl.ANY)
+    nfeat = lax.axis_size("feat")
     pieces = pl.pallas_call(
         functools.partial(arrange_kernel, outer),
         out_shape=(jax.ShapeDtypeStruct(((2 * outer + 1) * fcols, rows), jnp.bfloat16),) * (MERGE // 2),
-        in_specs=[any_spec] * 3,
-        out_specs=(any_spec,) * (MERGE // 2),
-        scratch_shapes=[pltpu.SemaphoreType.DMA((MERGE // 2, 2 * outer + 2))],
+        grid=(1,),
+        in_specs=[
+            pl.BlockSpec((fcols, rows * nfeat), lambda i: (0, 0)),
+            pl.BlockSpec((fcols, width), lambda i: (0, 0)),
+            pl.BlockSpec((fcols, width), lambda i: (0, 0)),
+        ],
+        out_specs=(pl.BlockSpec(((2 * outer + 1) * fcols, rows), lambda i: (0, 0)),) * (MERGE // 2),
+        compiler_params=pltpu.CompilerParams(vmem_limit_bytes=24 * 2**20),
         name="arrange",
     )(feats, w_self, w_neigh)
-    nfeat = lax.axis_size("feat")
     moved = [pieces[0]]
     for p in range(1, MERGE // 2):
         moved.append(lax.ppermute(pieces[p], "feat", [(f, f ^ (2 * p)) for f in range(nfeat)]))
@@ -209,49 +214,68 @@
 
     merged_cols = MERGE * fcols
 
-    def partial_pre(j):
+    part_rows = rows // PARTS
+
+    def partial_pre(j, c):
+        span = slice(c * part_rows, (c + 1) * part_rows)
         total = lax.dot_general(
-            xm[j].reshape(merged_cols, rows), wm[0].reshape(merged_cols, width),
+            xm[j, :, :, span].reshape(merged_cols, part_rows), wm[0].reshape(merged_cols, width),
             (((0,), (0,)), ((), ())), preferred_element_type=jnp.float32)
-        for copy in got[j]:
-            copy.wait_recv()
-        pending.extend(got[j])
+        if c == 0:
+            for copy in got[j]:
+                copy.wait_recv()
+            pending.extend(got[j])
         return total + lax.dot_general(
-            am[j].reshape(merged_cols, rows), wm[1].reshape(merged_cols, width),
+            am[j, :, :, span].reshape(merged_cols, part_rows), wm[1].reshape(merged_cols, width),
             (((0,), (0,)), ((), ())), preferred_element_type=jnp.float32)
 
-    sent = []
-    for j in range(1, outer):
-        psend[j] = partial_pre(j).astype(psend.dtype)
-        sent.append(remote(psend.at[j], precv.at[j], p_sems, (j,), outer_peer(j)))
-    pre = partial_pre(0) + bias_ref[...]
-    for j in range(1, outer):
-        sent[j - 1].wait_recv()
-        pre = pre + precv[j].astype(jnp.float32)
-    pending += sent
-    square = pre * pre
-    t = jnp.tanh(ROOT * pre * (1.0 + CUBIC * square))
-    half = 0.5 * (1.0 + t)
-    hidden_ref[...] = (pre * half).astype(hidden_ref.dtype)
-    slope = half + 0.5 * pre * (1.0 - t * t) * (ROOT * (1.0 + 3.0 * CUBIC * square))
-    dall[0] = (slope * up_ref[...].astype(jnp.float32)).astype(dall.dtype)
-    sent = [remote(dall.at[0], dall.at[j], d_sems, (j,), outer_peer(j)) for j in range(1, outer)]
-
-    colsum = jnp.zeros((1, width), jnp.float32)
-    for j in range(outer):
-        if j > 0:
-            sent[j - 1].wait_recv()
-        delta = dall[j]
-        colsum = colsum + jnp.sum(delta.astype(jnp.float32), axis=0, keepdims=True)
+    def grads(j, c, colsum):
+        span = slice(c * part_rows, (c + 1) * part_rows)
+        delta = dall[j, span]
         for i, merged in enumerate((xm, am)):
             part = jnp.dot(
-                merged[j].reshape(merged_cols, rows), delta, preferred_element_type=jnp.float32
+                merged[j, :, :, span].reshape(merged_cols, part_rows), delta,
+                preferred_element_type=jnp.float32,
             ).reshape(MERGE, fcols, width)
-            if j == 0:
+            if j == 0 and c == 0:
                 gacc[i] = part
             else:
                 gacc[i] = gacc[i] + part
-    pending += sent
+        return colsum + jnp.sum(delta.astype(jnp.float32), axis=0, keepdims=True)
+
+    sent = {}
+    for c in range(PARTS):
+        span = pl.ds(c * part_rows, part_rows)
+        for j in range(1, outer):
+            psend[j, span] = partial_pre(j, c).astype(psend.dtype)
+            sent[j, c] = remote(
+                psend.at[j, span], precv.at[j, span], p_sems, (j, c), outer_peer(j))
+    deltas = {}
+    for c in range(PARTS):
+        span = pl.ds(c * part_rows, part_rows)
+        pre = partial_pre(0, c) + bias_ref[...]
+        for j in range(1, outer):
+            sent[j, c].wait_recv()
+            pre = pre + precv[j, span].astype(jnp.float32)
+        square = pre * pre
+        t = jnp.tanh(ROOT * pre * (1.0 + CUBIC * square))
+        half = 0.5 * (1.0 + t)
+        slope = half + 0.5 * pre * (1.0 - t * t) * (ROOT * (1.0 + 3.0 * CUBIC * square))
+        dall[0, span] = (slope * up_ref[span].astype(jnp.float32)).astype(dall.dtype)
+        for j in range(1, outer):
+            deltas[j, c] = remote(
+                dall.at[0, span], dall.at[j, span], d_sems, (j, c), outer_peer(j))
+        hidden_ref[span] = (pre * half).astype(hidden_ref.dtype)
+    pending += list(sent.values())
+    pending += list(deltas.values())
+
+    colsum = jnp.zeros((1, width), jnp.float32)
+    for c in range(PARTS):
+        colsum = grads(0, c, colsum)
+    for c in range(PARTS):
+        for j in range(1, outer):
+            deltas[j, c].wait_recv()
+            colsum = grads(j, c, colsum)
     high = colsum.astype(jnp.bfloat16)
     low = (colsum - high.astype(jnp.float32)).astype(jnp.bfloat16)
     row_id = lax.broadcasted_iota(jnp.int32, (16, width), 0)
@@ -323,8 +347,8 @@
             pltpu.VMEM((groups, 2 * fcols + 16, width), jnp.float32),
             dma((2, outer, MERGE)),
             dma((2, MERGE // 2, outer + 2)),
-            dma((2, outer)),
-            dma((2, outer)),
+            dma((2, outer, PARTS)),
+            dma((2, outer, PARTS)),
             dma((2, MERGE)),
             dma((2, groups)),
             dma((MERGE // 2, outer + 2)),

time: 122 us -> 80 us (0.66)
  Pallas kernels: 110 us -> 65 us
  local copies, waits for them, and re-layouts: 5.49 us -> 8.59 us
    pallas_call x1, Pallas kernels: 41 us -> 0.15 us  [arrange(): pl.pallas_call(functools.partial(arrange_kernel, outer), out_shape=(jax.S...]
    pallas_call x1, Pallas kernels: 16.3 us -> 12.6 us  [aggregate(): pl.pallas_call(aggregate_kernel, grid_spec=pltpu.PrefetchScalarGridSpec(n...]
    unnamed x16 -> x20, local copies, waits for them, and re-layouts: 5.49 us -> 8.59 us
  transfers between devices with their start and end apart: 3 -> 3, of which waited for: 0 -> 0; matrix products, arithmetic and copies ran while one was open for 0% -> 0% of each run, Pallas kernels for 13% -> 16%
where the time goes in v4:
time: 80 us; the launch traced here: 79.6 us
  Pallas kernels  65 us (81%)
  local copies, waits for them, and re-layouts  8.59 us (11%)
  starting transfers between devices  4.61 us (6%)
  between operations  1.38 us (2%)
    pallas_call x1, Pallas kernels, exchange(): pl.pallas_call(functools.partial(exchange_kernel, groups, nfeat), out_sha...  52.2 us
    pallas_call x1, Pallas kernels, aggregate(): pl.pallas_call(aggregate_kernel, grid_spec=pltpu.PrefetchScalarGridSpec(n...  12.6 us
    unnamed x20, local copies, waits for them, and re-layouts  8.59 us
    ppermute x3, starting transfers between devices, arrange(): lax.ppermute(pieces[p], 'feat', [(f, f ^ 2 * p) for f in range(nfeat)])  4.61 us
  transfers between devices with their start and end apart: 3, of which 0 were waited for; matrix products, arithmetic and copies ran while one was open for 0% of the time, Pallas kernels for 16%

profile of v4, /device:TPU:0, one launch (start us, length us, event | category | flops | bytes accessed | tf_op | source)
XLA Modules:
  0.0 79.6 jit_solution(9570153099490870307)
XLA Ops:
  0.6 0.0 copy-start.7
  0.6 0.0 copy-start
  0.7 1.6 %copy-done = bf16[1,64,16384]{2,1,0:T(8,128)(2,1)S(1)} copy-done((bf16[1,64,16384]{2,1,0:T(8,128)(2,1)S(1)}, bf16[1,64,16384]{2,1,0:T(8,128)(2,1)}, u32[]{:S(2)}) %copy-start) | copy-done | bytes 2097176
  2.2 0.8 copy-done.3
  3.0 0.8 copy-done.4
  3.8 0.2 arrange.1
  3.9 3.0 %collective-permute-start = (bf16[320,512]{1,0:T(8,128)(2,1)S(1)}, bf16[320,512]{1,0:T(8,128)(2,1)S(1)}, u32[]{:S(2)}, u32[]{:S(2)}) collective-permute-start(bf16[320,512]{1,0:T(8,128)(2,1)S(1)} %get-tuple-element.13), channel_id=1, source_target_pairs={{0,2},{1,3},{2,0},{3,1},{4,6},{5,7},{6,4},{7,5},{8,10},{9,11},{10,... | collective-permute-start | bytes 983048 | tf_op jit(solution)/shard_map/ppermute | solution.py:132
  7.0 1.6 %collective-permute-start.1 = (bf16[320,512]{1,0:T(8,128)(2,1)S(1)}, bf16[320,512]{1,0:T(8,128)(2,1)S(1)}, u32[]{:S(2)}, u32[]{:S(2)}) collective-permute-start(bf16[320,512]{1,0:T(8,128)(2,1)S(1)} %get-tuple-element.14), channel_id=1, source_target_pairs={{0,4},{1,5},{2,6},{3,7},{4,0},{5,1},{6,2},{7,3},{8,12},{9,13},{10,... | collective-permute-start | bytes 983048 | tf_op jit(solution)/shard_map/ppermute | solution.py:132
  8.5 0.0 collective-permute-start.2
  9.2 0.0 copy-start.1
  9.2 1.6 %copy-done.1 = bf16[1,64,16384]{2,1,0:T(8,128)(2,1)S(1)} copy-done((bf16[1,64,16384]{2,1,0:T(8,128)(2,1)S(1)}, bf16[1,64,16384]{2,1,0:T(8,128)(2,1)}, u32[]{:S(2)}) %copy-start.1) | copy-done | bytes 2097176
  10.8 0.7 copy-done.5
  11.5 0.7 copy-done.6
  12.1 12.6 %aggregate.1.refs_4_ = bf16[64,8192]{1,0:T(8,128)(2,1)S(1)} custom-call(s32[512]{0:T(512)S(1)} %bitcast.8, s32[512]{0:T(512)S(1)} %bitcast.9, s32[1]{0:T(128)S(6)} %copy.17.count_ref, bf16[64,16384]{1,0:T(8,128)(2,1)S(1)} %bitcast.7, bf16[512,128,128]{2,1,0:T(8,128)(2,1)} %bitcast.12), custom_call_target="tpu_custom_call" | custom-call | flops 1073741824 | bytes 16777216 | tf_op jit(solution)/shard_map/aggregate/pallas_call | solution.py:67
  24.8 0.0 collective-permute-done.refs_1_
  24.8 0.0 collective-permute-done.1.refs_2_
  24.8 0.0 collective-permute-done.2.refs_3_
  24.8 0.0 copy-done.7
  24.8 0.0 copy-done.2
  24.8 52.2 %exchange.1 = (bf16[512,256]{1,0:T(8,128)(2,1)S(1)}, f32[64,256]{1,0:T(8,128)S(1)}, f32[64,256]{1,0:T(8,128)S(1)}, f32[1,256]{1,0:T(1,128)S(1)}) custom-call(bf16[320,512]{1,0:T(8,128)(2,1)S(1)} %get-tuple-element.12.refs_0_, bf16[320,512]{1,0:T(8,128)(2,1)S(1)} %collective-permute-done.refs_1_, bf16[320,512]{1,0:T(8,128)(2,1)S(1)} %collective-permute-done.1.refs_2_, ...), custom_call_target="tpu_custom_call" | custom-call | tf_op jit(solution)/shard_map/exchange/pallas_call | solution.py:326
  77.0 0.7 copy.18
  77.7 0.6 copy.19
  78.4 0.6 copy.20
  79.0 0.6 copy.21
  (5 shorter events, 0.0 us)
Async XLA Ops:
  0.6 24.2 %copy-start.7 = (f32[256]{0:T(256)S(1)}, f32[256]{0:T(256)}, u32[]{:S(2)}) copy-start(f32[256]{0:T(256)} %param.16) | copy-start | bytes 3076
  0.6 1.6 %copy-start = (bf16[1,64,16384]{2,1,0:T(8,128)(2,1)S(1)}, bf16[1,64,16384]{2,1,0:T(8,128)(2,1)}, u32[]{:S(2)}) copy-start(bf16[1,64,16384]{2,1,0:T(8,128)(2,1)} %param.9) | copy-start | bytes 6291460
  2.2 0.8 copy-start.3
  3.0 0.8 copy-start.4
  3.8 21.1 %copy-start.2 = (bf16[512,256]{1,0:T(8,128)(2,1)S(1)}, bf16[512,256]{1,0:T(8,128)(2,1)}, u32[]{:S(2)}) copy-start(bf16[512,256]{1,0:T(8,128)(2,1)} %refs_6_.1) | copy-start | bytes 786436
  3.9 20.9 %collective-permute-start = (bf16[320,512]{1,0:T(8,128)(2,1)S(1)}, bf16[320,512]{1,0:T(8,128)(2,1)S(1)}, u32[]{:S(2)}, u32[]{:S(2)}) collective-permute-start(bf16[320,512]{1,0:T(8,128)(2,1)S(1)} %get-tuple-element.13), channel_id=1, source_target_pairs={{0,2},{1,3},{2,0},{3,1},{4,6},{5,7},{6,4},{7,5},{8,10},{9,11},{10,... | collective-permute-start | bytes 983048 | tf_op jit(solution)/shard_map/ppermute | solution.py:132
  7.0 17.9 %collective-permute-start.1 = (bf16[320,512]{1,0:T(8,128)(2,1)S(1)}, bf16[320,512]{1,0:T(8,128)(2,1)S(1)}, u32[]{:S(2)}, u32[]{:S(2)}) collective-permute-start(bf16[320,512]{1,0:T(8,128)(2,1)S(1)} %get-tuple-element.14), channel_id=1, source_target_pairs={{0,4},{1,5},{2,6},{3,7},{4,0},{5,1},{6,2},{7,3},{8,12},{9,13},{10,... | collective-permute-start | bytes 983048 | tf_op jit(solution)/shard_map/ppermute | solution.py:132
  8.5 16.3 %collective-permute-start.2 = (bf16[320,512]{1,0:T(8,128)(2,1)S(1)}, bf16[320,512]{1,0:T(8,128)(2,1)S(1)}, u32[]{:S(2)}, u32[]{:S(2)}) collective-permute-start(bf16[320,512]{1,0:T(8,128)(2,1)S(1)} %get-tuple-element.15), channel_id=1, source_target_pairs={{0,6},{1,7},{2,4},{3,5},{4,2},{5,3},{6,0},{7,1},{8,14},{9,15},{10,... | collective-permute-start | bytes 983048 | tf_op jit(solution)/shard_map/ppermute | solution.py:132
  9.2 1.6 %copy-start.1 = (bf16[1,64,16384]{2,1,0:T(8,128)(2,1)S(1)}, bf16[1,64,16384]{2,1,0:T(8,128)(2,1)}, u32[]{:S(2)}) copy-start(bf16[1,64,16384]{2,1,0:T(8,128)(2,1)} %param.9) | copy-start | bytes 6291460
  10.8 0.7 copy-start.5
  11.5 0.7 copy-start.6

commit v5 on v4

--- a/solution.py
+++ b/solution.py
@@ -8,10 +8,10 @@
 from jax.sharding import PartitionSpec as P
 
 STEP = 64
-HALF = 16
-
-
-def aggregate_kernel(dst_ref, src_ref, count_ref, x_ref, w_ref, out_ref, acc_a, acc_b, buf_a, buf_b):
+UNROLL = 32
+
+
+def aggregate_kernel(dst_ref, src_ref, count_ref, x_ref, w_ref, out_ref, acc_a, acc_b):
     step = pl.program_id(0)
     tile = w_ref.shape[1]
     dtiles = out_ref.shape[1] // tile
@@ -21,42 +21,31 @@
     def _():
         acc_a[...] = jnp.zeros_like(acc_a)
         acc_b[...] = jnp.zeros_like(acc_b)
-        buf_b[...] = jnp.zeros_like(buf_b)
-
-    def multiply(first, buf):
-        for k in range(0, HALF, 2):
+
+    def place(i):
+        t = base + i
+        return jnp.where(t < count_ref[0], dst_ref[t], dtiles)
+
+    @pl.loop(0, STEP // UNROLL)
+    def _(group):
+        for k in range(0, UNROLL, 2):
+            i = group * UNROLL + k
             one, two = [
-                x_ref[:, pl.ds(pl.multiple_of(src_ref[base + first + k + n] * tile, tile), tile)]
+                x_ref[:, pl.ds(pl.multiple_of(src_ref[base + i + n] * tile, tile), tile)]
                 for n in range(2)
             ]
             zero = jnp.zeros_like(one)
             left = jnp.concatenate([
                 jnp.concatenate([one, zero], axis=1), jnp.concatenate([zero, two], axis=1)], axis=0)
-            right = jnp.concatenate([w_ref[first + k], w_ref[first + k + 1]], axis=1)
+            right = jnp.concatenate([w_ref[i], w_ref[i + 1]], axis=1)
             prod = lax.dot_general(
                 left, right, (((1,), (1,)), ((), ())), preferred_element_type=jnp.float32)
-            buf[k] = prod[:one.shape[0]]
-            buf[k + 1] = prod[one.shape[0]:]
-
-    def add(first, buf):
-        for k in range(HALF):
-            t = first + k
-            live = jnp.logical_and(t >= 0, t < count_ref[0])
-            d = jnp.where(live, dst_ref[jnp.maximum(t, 0)], dtiles)
-            acc = (acc_a, acc_b)[k % 2]
-            acc[d] = acc[d] + buf[k]
-
-    @pl.loop(0, STEP // (2 * HALF))
-    def _(pair):
-        first = pair * 2 * HALF
-        multiply(first, buf_a)
-        add(base + first - HALF, buf_b)
-        multiply(first + HALF, buf_b)
-        add(base + first, buf_a)
+            a, b = place(i), place(i + 1)
+            acc_a[a] = acc_a[a] + prod[:one.shape[0]]
+            acc_b[b] = acc_b[b] + prod[one.shape[0]:]
 
     @pl.when(step == pl.num_programs(0) - 1)
     def _():
-        add(base + STEP - HALF, buf_b)
         for d in range(dtiles):
             out_ref[:, d * tile:(d + 1) * tile] = (acc_a[d] + acc_b[d]).astype(out_ref.dtype)
 
@@ -74,11 +63,10 @@
                 pl.BlockSpec((STEP, tile, tile), lambda i, *_: (i, 0, 0)),
             ],
             out_specs=pl.BlockSpec((fcols, ndst), lambda i, *_: (0, 0), pipeline_mode=pl.Buffered(1)),
-            scratch_shapes=[pltpu.VMEM((ndst // tile + 1, fcols, tile), jnp.float32)] * 2
-            + [pltpu.VMEM((HALF, fcols, tile), jnp.float32)] * 2,
+            scratch_shapes=[pltpu.VMEM((ndst // tile + 1, fcols, tile), jnp.float32)] * 2,
         ),
         out_shape=jax.ShapeDtypeStruct((fcols, ndst), jnp.bfloat16),
-        compiler_params=pltpu.CompilerParams(vmem_limit_bytes=40 * 2**20),
+        compiler_params=pltpu.CompilerParams(vmem_limit_bytes=60 * 2**20),
         cost_estimate=pl.CostEstimate(
             flops=2 * total * fcols * tile * tile, bytes_accessed=total * tile * tile * 2,
             transcendentals=0,
@@ -124,7 +112,7 @@
             pl.BlockSpec((fcols, width), lambda i: (0, 0)),
         ],
         out_specs=(pl.BlockSpec(((2 * outer + 1) * fcols, rows), lambda i: (0, 0)),) * (MERGE // 2),
-        compiler_params=pltpu.CompilerParams(vmem_limit_bytes=24 * 2**20),
+        compiler_params=pltpu.CompilerParams(vmem_limit_bytes=60 * 2**20),
         name="arrange",
     )(feats, w_self, w_neigh)
     moved = [pieces[0]]
@@ -139,8 +127,8 @@
 ):
     moved, refs = refs[:MERGE // 2], refs[MERGE // 2:]
     a_ref, bias_ref, up_ref, hidden_ref, gs_ref, gn_ref, gb_ref, *refs = refs
-    xm, am, wm, psend, precv, dall, gacc, gsend, grecv, vsend, vrecv, *refs = refs
-    a_sems, s_sems, p_sems, d_sems, g_sems, v_sems, l_sems, own_sems = refs
+    xm, am, wm, psend, precv, dall, gacc, gsend, gpair, gout, grecv, vsend, vrecv, *refs = refs
+    a_sems, s_sems, p_sems, d_sems, h_sems, g_sems, v_sems, l_sems, own_sems = refs
     outer = nfeat // MERGE
     fcols = a_ref.shape[0]
     rows = up_ref.shape[0]
@@ -184,11 +172,14 @@
     pending = []
     local = []
     got = {}
-    for j in order:
+
+    def send_columns(j):
         got[j] = [
             remote(a_ref.at[:, columns(j, k)], am.at[j, k], a_sems, (j, k), inner_peer(k))
             for k in range(1, MERGE)
         ]
+
+    send_columns(order[0])
     for j in order:
         local.append(pltpu.make_async_copy(a_ref.at[:, columns(j, 0)], am.at[j, 0], own_sems.at[j]))
     shared = []
@@ -225,6 +216,8 @@
             for copy in got[j]:
                 copy.wait_recv()
             pending.extend(got[j])
+            if j > 0:
+                send_columns(order[order.index(j) + 1])
         return total + lax.dot_general(
             am[j, :, :, span].reshape(merged_cols, part_rows), wm[1].reshape(merged_cols, width),
             (((0,), (0,)), ((), ())), preferred_element_type=jnp.float32)
@@ -244,9 +237,9 @@
         return colsum + jnp.sum(delta.astype(jnp.float32), axis=0, keepdims=True)
 
     sent = {}
-    for c in range(PARTS):
-        span = pl.ds(c * part_rows, part_rows)
-        for j in range(1, outer):
+    for j in range(1, outer):
+        for c in range(PARTS):
+            span = pl.ds(c * part_rows, part_rows)
             psend[j, span] = partial_pre(j, c).astype(psend.dtype)
             sent[j, c] = remote(
                 psend.at[j, span], precv.at[j, span], p_sems, (j, c), outer_peer(j))
@@ -276,27 +269,47 @@
         for j in range(1, outer):
             deltas[j, c].wait_recv()
             colsum = grads(j, c, colsum)
-    high = colsum.astype(jnp.bfloat16)
-    low = (colsum - high.astype(jnp.float32)).astype(jnp.bfloat16)
     row_id = lax.broadcasted_iota(jnp.int32, (16, width), 0)
-    tag = jnp.where(
-        row_id == 0, high.astype(jnp.float32),
-        jnp.where(row_id == 1, low.astype(jnp.float32), 0.0)).astype(jnp.bfloat16)
-    sent = []
-    for k in range(1, MERGE):
-        gsend[k, 0:fcols] = gacc[0, k].astype(gsend.dtype)
-        gsend[k, fcols:2 * fcols] = gacc[1, k].astype(gsend.dtype)
-        gsend[k, 2 * fcols:2 * fcols + 16] = tag
-        sent.append(remote(gsend.at[k], grecv.at[k], g_sems, (k,), inner_peer(k)))
-    total_s = gacc[0, 0]
-    total_n = gacc[1, 0]
+    tail = slice(2 * fcols, 2 * fcols + 16)
+
+    def split(value):
+        high = value.astype(jnp.bfloat16).astype(jnp.float32)
+        return jnp.where(
+            row_id == 0, high, jnp.where(row_id == 1, value - high, 0.0)).astype(jnp.bfloat16)
+
+    def join(block):
+        return jnp.sum(block.astype(jnp.float32), axis=0, keepdims=True)
+
+    tag = split(colsum)
+    pairs = MERGE // 2
+    sent = {}
+    for m in list(range(1, pairs)) + [0]:
+        gsend[m, 0:fcols] = gacc[0, 2 * m + 1].astype(gsend.dtype)
+        gsend[m, fcols:2 * fcols] = gacc[1, 2 * m + 1].astype(gsend.dtype)
+        gsend[m, tail] = tag
+        sent[m] = remote(gsend.at[m], gpair.at[m], h_sems, (m,), inner_peer(1))
+    passed = {}
+    for m in range(1, pairs):
+        sent[m].wait_recv()
+        if m == 1:
+            colsum = colsum + join(gpair[1, tail])
+            tag = split(colsum)
+        gout[m, 0:fcols] = (gacc[0, 2 * m] + gpair[m, 0:fcols].astype(jnp.float32)).astype(gout.dtype)
+        gout[m, fcols:2 * fcols] = (
+            gacc[1, 2 * m] + gpair[m, fcols:2 * fcols].astype(jnp.float32)).astype(gout.dtype)
+        gout[m, tail] = tag
+        passed[m] = remote(gout.at[m], grecv.at[m], g_sems, (m,), inner_peer(2 * m))
+    sent[0].wait_recv()
+    total_s = gacc[0, 0] + gpair[0, 0:fcols].astype(jnp.float32)
+    total_n = gacc[1, 0] + gpair[0, fcols:2 * fcols].astype(jnp.float32)
+    for m in range(1, pairs):
+        passed[m].wait_recv()
+        total_s = total_s + grecv[m, 0:fcols].astype(jnp.float32)
+        total_n = total_n + grecv[m, fcols:2 * fcols].astype(jnp.float32)
+        colsum = colsum + join(grecv[m, tail])
     total_b = jnp.where(row_id == 0, colsum, 0.0)
-    for k in range(1, MERGE):
-        sent[k - 1].wait_recv()
-        total_s = total_s + grecv[k, 0:fcols].astype(jnp.float32)
-        total_n = total_n + grecv[k, fcols:2 * fcols].astype(jnp.float32)
-        total_b = total_b + grecv[k, 2 * fcols:2 * fcols + 16].astype(jnp.float32)
-    pending += sent
+    pending += list(sent.values())
+    pending += list(passed.values())
     vsend[0:fcols] = total_s
     vsend[fcols:2 * fcols] = total_n
     vsend[2 * fcols:2 * fcols + 16] = total_b
@@ -341,15 +354,18 @@
             pltpu.VMEM((outer, rows, width), jnp.bfloat16),
             pltpu.VMEM((outer, rows, width), jnp.bfloat16),
             pltpu.VMEM((2, MERGE, fcols, width), jnp.float32),
-            pltpu.VMEM((MERGE, 2 * fcols + 16, width), jnp.bfloat16),
-            pltpu.VMEM((MERGE, 2 * fcols + 16, width), jnp.bfloat16),
+            pltpu.VMEM((MERGE // 2, 2 * fcols + 16, width), jnp.bfloat16),
+            pltpu.VMEM((MERGE // 2, 2 * fcols + 16, width), jnp.bfloat16),
+            pltpu.VMEM((MERGE // 2, 2 * fcols + 16, width), jnp.bfloat16),
+            pltpu.VMEM((MERGE // 2, 2 * fcols + 16, width), jnp.bfloat16),
             pltpu.VMEM((2 * fcols + 16, width), jnp.float32),
             pltpu.VMEM((groups, 2 * fcols + 16, width), jnp.float32),
             dma((2, outer, MERGE)),
             dma((2, MERGE // 2, outer + 2)),
             dma((2, outer, PARTS)),
             dma((2, outer, PARTS)),
-            dma((2, MERGE)),
+            dma((2, MERGE // 2)),
+            dma((2, MERGE // 2)),
             dma((2, groups)),
             dma((MERGE // 2, outer + 2)),
             dma((outer,)),
@@ -360,6 +376,19 @@
     )(*moved, aggregated, bias.reshape(1, width), upstream)
 
 
+def finish_kernel(*refs):
+    for source, target in zip(refs[:4], refs[4:]):
+        target[...] = source[...]
+
+
+def finish(*parts):
+    return pl.pallas_call(
+        finish_kernel,
+        out_shape=tuple(jax.ShapeDtypeStruct(p.shape, p.dtype) for p in parts),
+        name="finish",
+    )(*parts)
+
+
 def body(
     features_t, tile_weights, tile_dst, tile_src, tile_count, w_self, w_neigh, bias, grad_hidden
 ):
@@ -367,7 +396,8 @@
     ndst = grad_hidden.shape[0] * lax.axis_size("feat")
     moved = arrange(feats, w_self, w_neigh, grad_hidden.shape[0])
     aggregated = aggregate(feats, tile_weights[0], tile_dst[0], tile_src[0], tile_count, ndst)
-    hidden, grad_self, grad_neigh, grad_bias = exchange(moved, aggregated, bias, grad_hidden)
+    hidden, grad_self, grad_neigh, grad_bias = finish(
+        *exchange(moved, aggregated, bias, grad_hidden))
     return (hidden, grad_self, grad_neigh, grad_bias[0])
 
 

time: 80 us -> 77.6 us (0.970)
  local copies, waits for them, and re-layouts: 8.59 us -> 3.72 us
  Pallas kernels: 65 us -> 67.6 us
    unnamed x20 -> x16, local copies, waits for them, and re-layouts: 8.59 us -> 3.72 us
    pallas_call x1, Pallas kernels: 52.2 us -> 49.1 us  [exchange(): pl.pallas_call(functools.partial(exchange_kernel, groups, nfeat), out_sha...]
    pallas_call x1, Pallas kernels: 0.15 us -> 2.45 us  [arrange(): pl.pallas_call(functools.partial(arrange_kernel, outer), out_shape=(jax.S...]
    pallas_call x0 -> x1, Pallas kernels: none -> 1.74 us  [finish(): pl.pallas_call(finish_kernel, out_shape=tuple((jax.ShapeDtypeStruct(p.sha...]
    pallas_call x1, Pallas kernels: 12.6 us -> 14.2 us  [aggregate(): pl.pallas_call(aggregate_kernel, grid_spec=pltpu.PrefetchScalarGridSpec(n...]
  transfers between devices with their start and end apart: 3 -> 3, of which waited for: 0 -> 0; matrix products, arithmetic and copies ran while one was open for 0% -> 0% of each run, Pallas kernels for 16% -> 18%
where the time goes in v5:
time: 77.6 us; the launch traced here: 77.2 us
  Pallas kernels  67.6 us (87%)
  starting transfers between devices  4.55 us (6%)
  local copies, waits for them, and re-layouts  3.72 us (5%)
  between operations  1.36 us (2%)
    pallas_call x1, Pallas kernels, exchange(): pl.pallas_call(functools.partial(exchange_kernel, groups, nfeat), out_sha...  49.1 us
    pallas_call x1, Pallas kernels, aggregate(): pl.pallas_call(aggregate_kernel, grid_spec=pltpu.PrefetchScalarGridSpec(n...  14.2 us
    ppermute x3, starting transfers between devices, arrange(): lax.ppermute(pieces[p], 'feat', [(f, f ^ 2 * p) for f in range(nfeat)])  4.55 us
    unnamed x16, local copies, waits for them, and re-layouts  3.72 us
    pallas_call x1, Pallas kernels, arrange(): pl.pallas_call(functools.partial(arrange_kernel, outer), out_shape=(jax.S...  2.45 us
    pallas_call x1, Pallas kernels, finish(): pl.pallas_call(finish_kernel, out_shape=tuple((jax.ShapeDtypeStruct(p.sha...  1.74 us
  transfers between devices with their start and end apart: 3, of which 0 were waited for; matrix products, arithmetic and copies ran while one was open for 0% of the time, Pallas kernels for 18%

profile of v5, /device:TPU:0, one launch (start us, length us, event | category | flops | bytes accessed | tf_op | source)
XLA Modules:
  0.0 77.2 jit_solution(12009565985967904564)
XLA Ops:
  0.6 0.0 copy-start.2
  0.6 0.0 copy-start.6
  0.7 2.5 %arrange.1 = (bf16[320,512]{1,0:T(8,128)(2,1)}, bf16[320,512]{1,0:T(8,128)(2,1)}, bf16[320,512]{1,0:T(8,128)(2,1)}, bf16[320,512]{1,0:T(8,128)(2,1)}) custom-call(bf16[64,16384]{1,0:T(8,128)(2,1)} %bitcast.8, bf16[64,256]{1,0:T(8,128)(2,1)} %ws_ref.1, bf16[64,256]{1,0:T(8,128)(2,1)} %wn_ref.1), custom_call_target="tpu_custom_call" | custom-call | tf_op jit(solution)/shard_map/arrange/pallas_call | solution.py:105
  3.1 0.0 copy-start.1
  3.1 3.0 %collective-permute-start = (bf16[320,512]{1,0:T(8,128)(2,1)}, bf16[320,512]{1,0:T(8,128)(2,1)S(1)}, u32[]{:S(2)}, u32[]{:S(2)}) collective-permute-start(bf16[320,512]{1,0:T(8,128)(2,1)} %get-tuple-element.17), channel_id=1, source_target_pairs={{0,2},{1,3},{2,0},{3,1},{4,6},{5,7},{6,4},{7,5},{8,10},{9,11},{10,... | collective-permute-start | bytes 983048 | tf_op jit(solution)/shard_map/ppermute | solution.py:120
  6.1 1.6 %collective-permute-start.1 = (bf16[320,512]{1,0:T(8,128)(2,1)}, bf16[320,512]{1,0:T(8,128)(2,1)S(1)}, u32[]{:S(2)}, u32[]{:S(2)}) collective-permute-start(bf16[320,512]{1,0:T(8,128)(2,1)} %get-tuple-element.18), channel_id=1, source_target_pairs={{0,4},{1,5},{2,6},{3,7},{4,0},{5,1},{6,2},{7,3},{8,12},{9,13},{10,... | collective-permute-start | bytes 983048 | tf_op jit(solution)/shard_map/ppermute | solution.py:120
  7.7 0.0 collective-permute-start.2
  8.3 14.2 %aggregate.1.refs_4_ = bf16[64,8192]{1,0:T(8,128)(2,1)} custom-call(s32[512]{0:T(512)} %bitcast.10, s32[512]{0:T(512)} %bitcast.11, s32[1]{0:T(128)S(6)} %copy.13.count_ref, bf16[64,16384]{1,0:T(8,128)(2,1)} %bitcast.9, bf16[512,128,128]{2,1,0:T(8,128)(2,1)} %bitcast.7), custom_call_target="tpu_custom_call" | custom-call | flops 1073741824 | bytes 16777216 | tf_op jit(solution)/shard_map/aggregate/pallas_call | solution.py:56
  22.5 0.0 collective-permute-done.refs_1_
  22.5 0.0 collective-permute-done.1.refs_2_
  22.5 0.0 collective-permute-done.2.refs_3_
  22.6 0.0 copy-done.2
  22.6 0.0 copy-done.6
  22.6 0.0 copy-done.1
  22.6 0.0 copy-start
  22.6 1.2 %copy-done = bf16[64,8192]{1,0:T(8,128)(2,1)S(1)} copy-done((bf16[64,8192]{1,0:T(8,128)(2,1)S(1)}, bf16[64,8192]{1,0:T(8,128)(2,1)}, u32[]{:S(2)}) %copy-start) | copy-done | bytes 1048600
  23.8 49.1 %exchange.1 = (bf16[512,256]{1,0:T(8,128)(2,1)S(1)}, f32[64,256]{1,0:T(8,128)S(1)}, f32[64,256]{1,0:T(8,128)S(1)}, f32[1,256]{1,0:T(1,128)S(1)}) custom-call(bf16[320,512]{1,0:T(8,128)(2,1)S(1)} %copy-done.1, bf16[320,512]{1,0:T(8,128)(2,1)S(1)} %collective-permute-done.refs_1_, bf16[320,512]{1,0:T(8,128)(2,1)S(1)} %collective-permute-done.1.refs_2_, ...), custom_call_target="tpu_custom_call" | custom-call | tf_op jit(solution)/shard_map/exchange/pallas_call | solution.py:339
  73.0 0.0 copy-start.3
  73.0 0.7 copy-done.3
  73.6 0.0 copy-start.4
  73.7 0.6 copy-done.4
  74.3 0.6 copy-done.5
  74.9 0.6 copy-done.7
  75.5 1.7 %finish.1 = (bf16[512,256]{1,0:T(8,128)(2,1)}, f32[64,256]{1,0:T(8,128)}, f32[64,256]{1,0:T(8,128)}, f32[1,256]{1,0:T(1,128)}) custom-call(bf16[512,256]{1,0:T(8,128)(2,1)} %copy-done.3, f32[64,256]{1,0:T(8,128)} %copy-done.4, f32[64,256]{1,0:T(8,128)} %copy-done.5, f32[1,256]{1,0:T(1,128)} %copy-done.7), custom_call_target="tpu_custom_call" | custom-call | tf_op jit(solution)/shard_map/finish/pallas_call | solution.py:385
  (2 shorter events, 0.0 us)
Async XLA Ops:
  0.6 21.9 %copy-start.2 = (bf16[512,256]{1,0:T(8,128)(2,1)S(1)}, bf16[512,256]{1,0:T(8,128)(2,1)}, u32[]{:S(2)}) copy-start(bf16[512,256]{1,0:T(8,128)(2,1)} %refs_6_.1) | copy-start | bytes 786436
  0.6 21.9 %copy-start.6 = (f32[256]{0:T(256)S(1)}, f32[256]{0:T(256)}, u32[]{:S(2)}) copy-start(f32[256]{0:T(256)} %param.16) | copy-start | bytes 3076
  3.1 19.5 %copy-start.1 = (bf16[320,512]{1,0:T(8,128)(2,1)S(1)}, bf16[320,512]{1,0:T(8,128)(2,1)}, u32[]{:S(2)}) copy-start(bf16[320,512]{1,0:T(8,128)(2,1)} %get-tuple-element.16.refs_0_) | copy-start | bytes 983044
  3.1 19.4 %collective-permute-start = (bf16[320,512]{1,0:T(8,128)(2,1)}, bf16[320,512]{1,0:T(8,128)(2,1)S(1)}, u32[]{:S(2)}, u32[]{:S(2)}) collective-permute-start(bf16[320,512]{1,0:T(8,128)(2,1)} %get-tuple-element.17), channel_id=1, source_target_pairs={{0,2},{1,3},{2,0},{3,1},{4,6},{5,7},{6,4},{7,5},{8,10},{9,11},{10,... | collective-permute-start | bytes 983048 | tf_op jit(solution)/shard_map/ppermute | solution.py:120
  6.1 16.5 %collective-permute-start.1 = (bf16[320,512]{1,0:T(8,128)(2,1)}, bf16[320,512]{1,0:T(8,128)(2,1)S(1)}, u32[]{:S(2)}, u32[]{:S(2)}) collective-permute-start(bf16[320,512]{1,0:T(8,128)(2,1)} %get-tuple-element.18), channel_id=1, source_target_pairs={{0,4},{1,5},{2,6},{3,7},{4,0},{5,1},{6,2},{7,3},{8,12},{9,13},{10,... | collective-permute-start | bytes 983048 | tf_op jit(solution)/shard_map/ppermute | solution.py:120
  7.7 14.9 %collective-permute-start.2 = (bf16[320,512]{1,0:T(8,128)(2,1)}, bf16[320,512]{1,0:T(8,128)(2,1)S(1)}, u32[]{:S(2)}, u32[]{:S(2)}) collective-permute-start(bf16[320,512]{1,0:T(8,128)(2,1)} %get-tuple-element.19), channel_id=1, source_target_pairs={{0,6},{1,7},{2,4},{3,5},{4,2},{5,3},{6,0},{7,1},{8,14},{9,15},{10,... | collective-permute-start | bytes 983048 | tf_op jit(solution)/shard_map/ppermute | solution.py:120
  22.6 1.2 %copy-start = (bf16[64,8192]{1,0:T(8,128)(2,1)S(1)}, bf16[64,8192]{1,0:T(8,128)(2,1)}, u32[]{:S(2)}) copy-start(bf16[64,8192]{1,0:T(8,128)(2,1)} %aggregate.1.refs_4_) | copy-start | bytes 3145732
  73.0 0.7 copy-start.3
  73.6 0.6 copy-start.4
  74.3 0.6 copy-start.5
  74.9 0.6 copy-start.7

commit v6 on v5

--- a/solution.py
+++ b/solution.py
@@ -16,6 +16,7 @@
     tile = w_ref.shape[1]
     dtiles = out_ref.shape[1] // tile
     base = step * STEP
+    fcols = x_ref.shape[0]
 
     @pl.when(step == 0)
     def _():
@@ -28,21 +29,26 @@
 
     @pl.loop(0, STEP // UNROLL)
     def _(group):
-        for k in range(0, UNROLL, 2):
+        for k in range(0, UNROLL, 4):
             i = group * UNROLL + k
-            one, two = [
+            cols = [
                 x_ref[:, pl.ds(pl.multiple_of(src_ref[base + i + n] * tile, tile), tile)]
-                for n in range(2)
+                for n in range(4)
             ]
-            zero = jnp.zeros_like(one)
+            zero = jnp.zeros_like(cols[0])
             left = jnp.concatenate([
-                jnp.concatenate([one, zero], axis=1), jnp.concatenate([zero, two], axis=1)], axis=0)
-            right = jnp.concatenate([w_ref[i], w_ref[i + 1]], axis=1)
+                jnp.concatenate([cols[n], zero] if n % 2 == 0 else [zero, cols[n]], axis=1)
+                for n in range(4)], axis=0)
+            right = jnp.concatenate([
+                jnp.concatenate([w_ref[i], w_ref[i + 1]], axis=1),
+                jnp.concatenate([w_ref[i + 2], w_ref[i + 3]], axis=1)], axis=0)
             prod = lax.dot_general(
                 left, right, (((1,), (1,)), ((), ())), preferred_element_type=jnp.float32)
-            a, b = place(i), place(i + 1)
-            acc_a[a] = acc_a[a] + prod[:one.shape[0]]
-            acc_b[b] = acc_b[b] + prod[one.shape[0]:]
+            for n in range(4):
+                d = place(i + n)
+                acc = (acc_a, acc_b)[n % 2]
+                half = n // 2 * tile
+                acc[d] = acc[d] + prod[n * fcols:(n + 1) * fcols, half:half + tile]
 
     @pl.when(step == pl.num_programs(0) - 1)
     def _():
@@ -173,13 +179,19 @@
     local = []
     got = {}
 
-    def send_columns(j):
-        got[j] = [
-            remote(a_ref.at[:, columns(j, k)], am.at[j, k], a_sems, (j, k), inner_peer(k))
-            for k in range(1, MERGE)
-        ]
-
-    send_columns(order[0])
+    steps = [(j, c) for j in order for c in range(PARTS)]
+    part_rows = rows // PARTS
+
+    def send_columns(j, c):
+        got[j, c] = []
+        for k in range(1, MERGE):
+            owner = (hi ^ j) * MERGE + (lo ^ k)
+            source = pl.ds(pl.multiple_of(owner * rows + c * part_rows, part_rows), part_rows)
+            got[j, c].append(remote(
+                a_ref.at[:, source], am.at[j, k, :, pl.ds(c * part_rows, part_rows)],
+                a_sems, (j, c, k), inner_peer(k)))
+
+    send_columns(*steps[0])
     for j in order:
         local.append(pltpu.make_async_copy(a_ref.at[:, columns(j, 0)], am.at[j, 0], own_sems.at[j]))
     shared = []
@@ -205,19 +217,18 @@
 
     merged_cols = MERGE * fcols
 
-    part_rows = rows // PARTS
-
     def partial_pre(j, c):
         span = slice(c * part_rows, (c + 1) * part_rows)
         total = lax.dot_general(
             xm[j, :, :, span].reshape(merged_cols, part_rows), wm[0].reshape(merged_cols, width),
             (((0,), (0,)), ((), ())), preferred_element_type=jnp.float32)
-        if c == 0:
-            for copy in got[j]:
-                copy.wait_recv()
-            pending.extend(got[j])
-            if j > 0:
-                send_columns(order[order.index(j) + 1])
+        for copy in got[j, c]:
+            copy.wait_recv()
+        pending.extend(got[j, c])
+        if j > 0:
+            later = steps.index((j, c)) + 1
+            for step in steps[later:later + 1] if steps[later][0] > 0 else steps[later:]:
+                send_columns(*step)
         return total + lax.dot_general(
             am[j, :, :, span].reshape(merged_cols, part_rows), wm[1].reshape(merged_cols, width),
             (((0,), (0,)), ((), ())), preferred_element_type=jnp.float32)
@@ -307,22 +318,21 @@
         total_s = total_s + grecv[m, 0:fcols].astype(jnp.float32)
         total_n = total_n + grecv[m, fcols:2 * fcols].astype(jnp.float32)
         colsum = colsum + join(grecv[m, tail])
-    total_b = jnp.where(row_id == 0, colsum, 0.0)
     pending += list(sent.values())
     pending += list(passed.values())
-    vsend[0:fcols] = total_s
-    vsend[fcols:2 * fcols] = total_n
-    vsend[2 * fcols:2 * fcols + 16] = total_b
+    vsend[0:fcols] = total_s.astype(vsend.dtype)
+    vsend[fcols:2 * fcols] = total_n.astype(vsend.dtype)
+    vsend[tail] = split(colsum)
     sent = [remote(vsend, vrecv.at[j], v_sems, (j,), group_peer(j)) for j in range(1, groups)]
     for j in range(1, groups):
         sent[j - 1].wait_recv()
-        total_s = total_s + vrecv[j, 0:fcols]
-        total_n = total_n + vrecv[j, fcols:2 * fcols]
-        total_b = total_b + vrecv[j, 2 * fcols:2 * fcols + 16]
+        total_s = total_s + vrecv[j, 0:fcols].astype(jnp.float32)
+        total_n = total_n + vrecv[j, fcols:2 * fcols].astype(jnp.float32)
+        colsum = colsum + join(vrecv[j, tail])
     pending += sent
     gs_ref[...] = total_s
     gn_ref[...] = total_n
-    gb_ref[...] = jnp.sum(total_b, axis=0, keepdims=True)
+    gb_ref[...] = colsum
     for copy in pending:
         copy.wait_send()
 
@@ -358,9 +368,9 @@
             pltpu.VMEM((MERGE // 2, 2 * fcols + 16, width), jnp.bfloat16),
             pltpu.VMEM((MERGE // 2, 2 * fcols + 16, width), jnp.bfloat16),
             pltpu.VMEM((MERGE // 2, 2 * fcols + 16, width), jnp.bfloat16),
-            pltpu.VMEM((2 * fcols + 16, width), jnp.float32),
-            pltpu.VMEM((groups, 2 * fcols + 16, width), jnp.float32),
-            dma((2, outer, MERGE)),
+            pltpu.VMEM((2 * fcols + 16, width), jnp.bfloat16),
+            pltpu.VMEM((groups, 2 * fcols + 16, width), jnp.bfloat16),
+            dma((2, outer, PARTS, MERGE)),
             dma((2, MERGE // 2, outer + 2)),
             dma((2, outer, PARTS)),
             dma((2, outer, PARTS)),
@@ -371,22 +381,9 @@
             dma((outer,)),
         ],
         compiler_params=pltpu.CompilerParams(
-            collective_id=0, has_side_effects=True, vmem_limit_bytes=40 * 2**20),
+            collective_id=0, has_side_effects=True, vmem_limit_bytes=62 * 2**20),
         name="exchange",
     )(*moved, aggregated, bias.reshape(1, width), upstream)
-
-
-def finish_kernel(*refs):
-    for source, target in zip(refs[:4], refs[4:]):
-        target[...] = source[...]
-
-
-def finish(*parts):
-    return pl.pallas_call(
-        finish_kernel,
-        out_shape=tuple(jax.ShapeDtypeStruct(p.shape, p.dtype) for p in parts),
-        name="finish",
-    )(*parts)
 
 
 def body(
@@ -396,8 +393,7 @@
     ndst = grad_hidden.shape[0] * lax.axis_size("feat")
     moved = arrange(feats, w_self, w_neigh, grad_hidden.shape[0])
     aggregated = aggregate(feats, tile_weights[0], tile_dst[0], tile_src[0], tile_count, ndst)
-    hidden, grad_self, grad_neigh, grad_bias = finish(
-        *exchange(moved, aggregated, bias, grad_hidden))
+    hidden, grad_self, grad_neigh, grad_bias = exchange(moved, aggregated, bias, grad_hidden)
     return (hidden, grad_self, grad_neigh, grad_bias[0])
 
 

time: 77.6 us -> 81.5 us (1.050)
  local copies, waits for them, and re-layouts: 3.72 us -> 6.75 us
    unnamed x16 -> x10, local copies, waits for them, and re-layouts: 3.72 us -> 6.75 us
    pallas_call x1, Pallas kernels: 49.1 us -> 51.4 us  [exchange(): pl.pallas_call(functools.partial(exchange_kernel, groups, nfeat), out_sha...]
    pallas_call x1 -> x0, Pallas kernels: 1.74 us -> none  [finish(): pl.pallas_call(finish_kernel, out_shape=tuple((jax.ShapeDtypeStruct(p.sha...]
where the time goes in v6:
time: 81.5 us; the launch traced here: 80.9 us
  Pallas kernels  68.3 us (84%)
  local copies, waits for them, and re-layouts  6.75 us (8%)
  starting transfers between devices  4.55 us (6%)
  between operations  1.32 us (2%)
    pallas_call x1, Pallas kernels, exchange(): pl.pallas_call(functools.partial(exchange_kernel, groups, nfeat), out_sha...  51.4 us
    pallas_call x1, Pallas kernels, aggregate(): pl.pallas_call(aggregate_kernel, grid_spec=pltpu.PrefetchScalarGridSpec(n...  14.5 us
    unnamed x10, local copies, waits for them, and re-layouts  6.75 us
    ppermute x3, starting transfers between devices, arrange(): lax.ppermute(pieces[p], 'feat', [(f, f ^ 2 * p) for f in range(nfeat)])  4.55 us
    pallas_call x1, Pallas kernels, arrange(): pl.pallas_call(functools.partial(arrange_kernel, outer), out_shape=(jax.S...  2.41 us
  transfers between devices with their start and end apart: 3, of which 0 were waited for; matrix products, arithmetic and copies ran while one was open for 0% of the time, Pallas kernels for 18%

profile of v6, /device:TPU:0, one launch (start us, length us, event | category | flops | bytes accessed | tf_op | source)
XLA Modules:
  0.0 80.9 jit_solution(9300200268701920112)
XLA Ops:
  0.6 2.4 %arrange.1 = (bf16[320,512]{1,0:T(8,128)(2,1)}, bf16[320,512]{1,0:T(8,128)(2,1)}, bf16[320,512]{1,0:T(8,128)(2,1)}, bf16[320,512]{1,0:T(8,128)(2,1)}) custom-call(bf16[64,16384]{1,0:T(8,128)(2,1)} %bitcast.7, bf16[64,256]{1,0:T(8,128)(2,1)} %ws_ref.1, bf16[64,256]{1,0:T(8,128)(2,1)} %wn_ref.1), custom_call_target="tpu_custom_call" | custom-call | tf_op jit(solution)/shard_map/arrange/pallas_call | solution.py:111
  3.0 3.0 %collective-permute-start = (bf16[320,512]{1,0:T(8,128)(2,1)}, bf16[320,512]{1,0:T(8,128)(2,1)S(1)}, u32[]{:S(2)}, u32[]{:S(2)}) collective-permute-start(bf16[320,512]{1,0:T(8,128)(2,1)} %get-tuple-element.13), channel_id=1, source_target_pairs={{0,2},{1,3},{2,0},{3,1},{4,6},{5,7},{6,4},{7,5},{8,10},{9,11},{10,... | collective-permute-start | bytes 983048 | tf_op jit(solution)/shard_map/ppermute | solution.py:126
  6.0 1.6 %collective-permute-start.1 = (bf16[320,512]{1,0:T(8,128)(2,1)}, bf16[320,512]{1,0:T(8,128)(2,1)S(1)}, u32[]{:S(2)}, u32[]{:S(2)}) collective-permute-start(bf16[320,512]{1,0:T(8,128)(2,1)} %get-tuple-element.14), channel_id=1, source_target_pairs={{0,4},{1,5},{2,6},{3,7},{4,0},{5,1},{6,2},{7,3},{8,12},{9,13},{10,... | collective-permute-start | bytes 983048 | tf_op jit(solution)/shard_map/ppermute | solution.py:126
  7.6 0.0 collective-permute-start.2
  8.2 14.5 %aggregate.1.refs_4_ = bf16[64,8192]{1,0:T(8,128)(2,1)} custom-call(s32[512]{0:T(512)} %bitcast.9, s32[512]{0:T(512)} %bitcast.10, s32[1]{0:T(128)S(6)} %copy.17.count_ref, bf16[64,16384]{1,0:T(8,128)(2,1)} %bitcast.8, bf16[512,128,128]{2,1,0:T(8,128)(2,1)} %bitcast.6), custom_call_target="tpu_custom_call" | custom-call | flops 1073741824 | bytes 16777216 | tf_op jit(solution)/shard_map/aggregate/pallas_call | solution.py:62
  22.8 0.0 collective-permute-done.refs_1_
  22.8 0.0 copy-start
  22.8 0.0 collective-permute-done.1.refs_2_
  22.8 0.0 copy-start.1
  22.8 0.0 collective-permute-done.2.refs_3_
  22.8 0.0 copy-start.2
  22.8 0.7 copy-done
  23.5 0.1 copy-done.1
  23.6 0.1 copy-done.2
  23.7 51.4 %exchange.1 = (bf16[512,256]{1,0:T(8,128)(2,1)}, f32[64,256]{1,0:T(8,128)}, f32[64,256]{1,0:T(8,128)}, f32[1,256]{1,0:T(1,128)}) custom-call(bf16[320,512]{1,0:T(8,128)(2,1)} %get-tuple-element.12.refs_0_, bf16[320,512]{1,0:T(8,128)(2,1)} %copy-done, bf16[320,512]{1,0:T(8,128)(2,1)} %copy-done.1, bf16[320,512]{1,0:T(8,128)(2,1)} %copy-done.2, ...), custom_call_target="tpu_custom_call" | custom-call | tf_op jit(solution)/shard_map/exchange/pallas_call | solution.py:349
  75.1 1.7 %copy.18 = bf16[512,256]{1,0:T(8,128)(2,1)} copy(bf16[512,256]{1,0:T(8,128)(2,1)} %get-tuple-element.24) | data formatting | bytes 524288
  76.8 1.5 %copy.19 = f32[64,256]{1,0:T(8,128)} copy(f32[64,256]{1,0:T(8,128)} %get-tuple-element.25) | data formatting | bytes 131072
  78.2 1.5 %copy.20 = f32[64,256]{1,0:T(8,128)} copy(f32[64,256]{1,0:T(8,128)} %get-tuple-element.26) | data formatting | bytes 131072
  79.7 1.2 %copy.21 = f32[256]{0:T(256)} copy(f32[256]{0:T(256)} %bitcast.12) | data formatting | bytes 2048
Async XLA Ops:
  3.0 19.7 %collective-permute-start = (bf16[320,512]{1,0:T(8,128)(2,1)}, bf16[320,512]{1,0:T(8,128)(2,1)S(1)}, u32[]{:S(2)}, u32[]{:S(2)}) collective-permute-start(bf16[320,512]{1,0:T(8,128)(2,1)} %get-tuple-element.13), channel_id=1, source_target_pairs={{0,2},{1,3},{2,0},{3,1},{4,6},{5,7},{6,4},{7,5},{8,10},{9,11},{10,... | collective-permute-start | bytes 983048 | tf_op jit(solution)/shard_map/ppermute | solution.py:126
  6.0 16.8 %collective-permute-start.1 = (bf16[320,512]{1,0:T(8,128)(2,1)}, bf16[320,512]{1,0:T(8,128)(2,1)S(1)}, u32[]{:S(2)}, u32[]{:S(2)}) collective-permute-start(bf16[320,512]{1,0:T(8,128)(2,1)} %get-tuple-element.14), channel_id=1, source_target_pairs={{0,4},{1,5},{2,6},{3,7},{4,0},{5,1},{6,2},{7,3},{8,12},{9,13},{10,... | collective-permute-start | bytes 983048 | tf_op jit(solution)/shard_map/ppermute | solution.py:126
  7.6 15.2 %collective-permute-start.2 = (bf16[320,512]{1,0:T(8,128)(2,1)}, bf16[320,512]{1,0:T(8,128)(2,1)S(1)}, u32[]{:S(2)}, u32[]{:S(2)}) collective-permute-start(bf16[320,512]{1,0:T(8,128)(2,1)} %get-tuple-element.15), channel_id=1, source_target_pairs={{0,6},{1,7},{2,4},{3,5},{4,2},{5,3},{6,0},{7,1},{8,14},{9,15},{10,... | collective-permute-start | bytes 983048 | tf_op jit(solution)/shard_map/ppermute | solution.py:126
  22.8 0.7 copy-start
  22.8 0.8 %copy-start.1 = (bf16[320,512]{1,0:T(8,128)(2,1)}, bf16[320,512]{1,0:T(8,128)(2,1)S(1)}, u32[]{:S(2)}) copy-start(bf16[320,512]{1,0:T(8,128)(2,1)S(1)} %collective-permute-done.1.refs_2_) | copy-start | bytes 983044
  22.8 0.9 %copy-start.2 = (bf16[320,512]{1,0:T(8,128)(2,1)}, bf16[320,512]{1,0:T(8,128)(2,1)S(1)}, u32[]{:S(2)}) copy-start(bf16[320,512]{1,0:T(8,128)(2,1)S(1)} %collective-permute-done.2.refs_3_) | copy-start | bytes 983044

commit v7 on v5

--- a/solution.py
+++ b/solution.py
@@ -7,64 +7,79 @@
 from jax.experimental.pallas import tpu as pltpu
 from jax.sharding import PartitionSpec as P
 
-STEP = 64
-UNROLL = 32
-
-
-def aggregate_kernel(dst_ref, src_ref, count_ref, x_ref, w_ref, out_ref, acc_a, acc_b):
-    step = pl.program_id(0)
-    tile = w_ref.shape[1]
+STEP = 32
+PACK = 16
+
+
+def aggregate_kernel(
+    dst_ref, src_ref, count_ref, x_any, w_any, out_ref, x_ref, w_ref, acc_a, acc_b, x_sems, w_sems
+):
+    fcols = x_any.shape[0]
+    total, tile, _ = w_any.shape
     dtiles = out_ref.shape[1] // tile
-    base = step * STEP
-
-    @pl.when(step == 0)
-    def _():
-        acc_a[...] = jnp.zeros_like(acc_a)
-        acc_b[...] = jnp.zeros_like(acc_b)
-
-    def place(i):
-        t = base + i
+
+    x_copies = [
+        pltpu.make_async_copy(
+            x_any.at[pl.ds(q * PACK, PACK)], x_ref.at[pl.ds(q * PACK, PACK)], x_sems.at[q])
+        for q in range(fcols // PACK)
+    ]
+
+    def w_copy(step):
+        span = pl.ds(step * STEP, STEP)
+        return pltpu.make_async_copy(w_any.at[span], w_ref.at[span], w_sems.at[step])
+
+    for copy in x_copies:
+        copy.start()
+    for step in range(total // STEP):
+        w_copy(step).start()
+    acc_a[...] = jnp.zeros_like(acc_a)
+    acc_b[...] = jnp.zeros_like(acc_b)
+    for copy in x_copies:
+        copy.wait()
+
+    def place(t):
         return jnp.where(t < count_ref[0], dst_ref[t], dtiles)
 
-    @pl.loop(0, STEP // UNROLL)
-    def _(group):
-        for k in range(0, UNROLL, 2):
-            i = group * UNROLL + k
+    @pl.loop(0, total // STEP)
+    def _(step):
+        w_copy(step).wait()
+        for k in range(0, STEP, 2):
+            t = step * STEP + k
             one, two = [
-                x_ref[:, pl.ds(pl.multiple_of(src_ref[base + i + n] * tile, tile), tile)]
+                x_ref[:, pl.ds(pl.multiple_of(src_ref[t + n] * tile, tile), tile)]
                 for n in range(2)
             ]
             zero = jnp.zeros_like(one)
             left = jnp.concatenate([
                 jnp.concatenate([one, zero], axis=1), jnp.concatenate([zero, two], axis=1)], axis=0)
-            right = jnp.concatenate([w_ref[i], w_ref[i + 1]], axis=1)
+            right = jnp.concatenate([w_ref[t], w_ref[t + 1]], axis=1)
             prod = lax.dot_general(
                 left, right, (((1,), (1,)), ((), ())), preferred_element_type=jnp.float32)
-            a, b = place(i), place(i + 1)
-            acc_a[a] = acc_a[a] + prod[:one.shape[0]]
-            acc_b[b] = acc_b[b] + prod[one.shape[0]:]
-
-    @pl.when(step == pl.num_programs(0) - 1)
-    def _():
-        for d in range(dtiles):
-            out_ref[:, d * tile:(d + 1) * tile] = (acc_a[d] + acc_b[d]).astype(out_ref.dtype)
+            a, b = place(t), place(t + 1)
+            acc_a[a] = acc_a[a] + prod[:fcols]
+            acc_b[b] = acc_b[b] + prod[fcols:]
+
+    for d in range(dtiles):
+        out_ref[:, d * tile:(d + 1) * tile] = (acc_a[d] + acc_b[d]).astype(out_ref.dtype)
 
 
 def aggregate(feats, tiles, dsts, srcs, count, ndst):
     fcols, nsrc = feats.shape
     total, tile, _ = tiles.shape
+    smem = pl.BlockSpec(memory_space=pltpu.SMEM)
+    any_spec = pl.BlockSpec(memory_space=pl.ANY)
     return pl.pallas_call(
         aggregate_kernel,
-        grid_spec=pltpu.PrefetchScalarGridSpec(
-            num_scalar_prefetch=3,
-            grid=(total // STEP,),
-            in_specs=[
-                pl.BlockSpec((fcols, nsrc), lambda i, *_: (0, 0), pipeline_mode=pl.Buffered(1)),
-                pl.BlockSpec((STEP, tile, tile), lambda i, *_: (i, 0, 0)),
-            ],
-            out_specs=pl.BlockSpec((fcols, ndst), lambda i, *_: (0, 0), pipeline_mode=pl.Buffered(1)),
-            scratch_shapes=[pltpu.VMEM((ndst // tile + 1, fcols, tile), jnp.float32)] * 2,
-        ),
+        in_specs=[smem, smem, smem, any_spec, any_spec],
+        out_specs=pl.BlockSpec(memory_space=pltpu.VMEM),
+        scratch_shapes=[
+            pltpu.VMEM((fcols, nsrc), jnp.bfloat16),
+            pltpu.VMEM((total, tile, tile), jnp.bfloat16),
+            pltpu.VMEM((ndst // tile + 1, fcols, tile), jnp.float32),
+            pltpu.VMEM((ndst // tile + 1, fcols, tile), jnp.float32),
+            pltpu.SemaphoreType.DMA((fcols // PACK,)),
+            pltpu.SemaphoreType.DMA((total // STEP,)),
+        ],
         out_shape=jax.ShapeDtypeStruct((fcols, ndst), jnp.bfloat16),
         compiler_params=pltpu.CompilerParams(vmem_limit_bytes=60 * 2**20),
         cost_estimate=pl.CostEstimate(
@@ -81,9 +96,10 @@
 ROOT = 0.7978845608
 
 
-def arrange_kernel(outer, x_ref, ws_ref, wn_ref, *refs):
-    outs = refs
+def arrange_kernel(outer, ws_ref, wn_ref, *refs):
     fcols, width = ws_ref.shape
+    bands = fcols // PACK
+    x_refs, outs = refs[:bands], refs[bands:]
     rows = outs[0].shape[1]
     me = lax.axis_index("feat")
     for p, out in enumerate(outs):
@@ -91,30 +107,31 @@
             for j in range(outer):
                 owner = me ^ (j * MERGE + 2 * p + side)
                 columns = pl.ds(pl.multiple_of(owner * rows, rows), rows)
-                place = side * outer + j
-                out[place * fcols:(place + 1) * fcols] = x_ref[:, columns]
+                for q in range(bands):
+                    first = (side * outer + j) * fcols + q * PACK
+                    out[first:first + PACK] = x_refs[q][:, columns]
         last = slice(2 * outer * fcols, (2 * outer + 1) * fcols)
         out[last, 0:width] = ws_ref[...]
         out[last, width:2 * width] = wn_ref[...]
 
 
 def arrange(feats, w_self, w_neigh, rows):
-    outer = lax.axis_size("feat") // MERGE
+    nfeat = lax.axis_size("feat")
+    outer = nfeat // MERGE
     fcols, width = w_self.shape
-    nfeat = lax.axis_size("feat")
+    bands = fcols // PACK
+    whole = pl.BlockSpec((fcols, width), lambda i: (0, 0))
     pieces = pl.pallas_call(
         functools.partial(arrange_kernel, outer),
-        out_shape=(jax.ShapeDtypeStruct(((2 * outer + 1) * fcols, rows), jnp.bfloat16),) * (MERGE // 2),
+        out_shape=(
+            jax.ShapeDtypeStruct(((2 * outer + 1) * fcols, rows), jnp.bfloat16),) * (MERGE // 2),
         grid=(1,),
-        in_specs=[
-            pl.BlockSpec((fcols, rows * nfeat), lambda i: (0, 0)),
-            pl.BlockSpec((fcols, width), lambda i: (0, 0)),
-            pl.BlockSpec((fcols, width), lambda i: (0, 0)),
-        ],
+        in_specs=[whole, whole] + [
+            pl.BlockSpec((PACK, rows * nfeat), lambda i, q=q: (q, 0)) for q in range(bands)],
         out_specs=(pl.BlockSpec(((2 * outer + 1) * fcols, rows), lambda i: (0, 0)),) * (MERGE // 2),
         compiler_params=pltpu.CompilerParams(vmem_limit_bytes=60 * 2**20),
         name="arrange",
-    )(feats, w_self, w_neigh)
+    )(w_self, w_neigh, *[feats] * bands)
     moved = [pieces[0]]
     for p in range(1, MERGE // 2):
         moved.append(lax.ppermute(pieces[p], "feat", [(f, f ^ (2 * p)) for f in range(nfeat)]))
@@ -307,22 +324,21 @@
         total_s = total_s + grecv[m, 0:fcols].astype(jnp.float32)
         total_n = total_n + grecv[m, fcols:2 * fcols].astype(jnp.float32)
         colsum = colsum + join(grecv[m, tail])
-    total_b = jnp.where(row_id == 0, colsum, 0.0)
     pending += list(sent.values())
     pending += list(passed.values())
-    vsend[0:fcols] = total_s
-    vsend[fcols:2 * fcols] = total_n
-    vsend[2 * fcols:2 * fcols + 16] = total_b
+    vsend[0:fcols] = total_s.astype(vsend.dtype)
+    vsend[fcols:2 * fcols] = total_n.astype(vsend.dtype)
+    vsend[tail] = split(colsum)
     sent = [remote(vsend, vrecv.at[j], v_sems, (j,), group_peer(j)) for j in range(1, groups)]
     for j in range(1, groups):
         sent[j - 1].wait_recv()
-        total_s = total_s + vrecv[j, 0:fcols]
-        total_n = total_n + vrecv[j, fcols:2 * fcols]
-        total_b = total_b + vrecv[j, 2 * fcols:2 * fcols + 16]
+        total_s = total_s + vrecv[j, 0:fcols].astype(jnp.float32)
+        total_n = total_n + vrecv[j, fcols:2 * fcols].astype(jnp.float32)
+        colsum = colsum + join(vrecv[j, tail])
     pending += sent
     gs_ref[...] = total_s
     gn_ref[...] = total_n
-    gb_ref[...] = jnp.sum(total_b, axis=0, keepdims=True)
+    gb_ref[...] = colsum
     for copy in pending:
         copy.wait_send()
 
@@ -358,8 +374,8 @@
             pltpu.VMEM((MERGE // 2, 2 * fcols + 16, width), jnp.bfloat16),
             pltpu.VMEM((MERGE // 2, 2 * fcols + 16, width), jnp.bfloat16),
             pltpu.VMEM((MERGE // 2, 2 * fcols + 16, width), jnp.bfloat16),
-            pltpu.VMEM((2 * fcols + 16, width), jnp.float32),
-            pltpu.VMEM((groups, 2 * fcols + 16, width), jnp.float32),
+            pltpu.VMEM((2 * fcols + 16, width), jnp.bfloat16),
+            pltpu.VMEM((groups, 2 * fcols + 16, width), jnp.bfloat16),
             dma((2, outer, MERGE)),
             dma((2, MERGE // 2, outer + 2)),
             dma((2, outer, PARTS)),
@@ -376,19 +392,6 @@
     )(*moved, aggregated, bias.reshape(1, width), upstream)
 
 
-def finish_kernel(*refs):
-    for source, target in zip(refs[:4], refs[4:]):
-        target[...] = source[...]
-
-
-def finish(*parts):
-    return pl.pallas_call(
-        finish_kernel,
-        out_shape=tuple(jax.ShapeDtypeStruct(p.shape, p.dtype) for p in parts),
-        name="finish",
-    )(*parts)
-
-
 def body(
     features_t, tile_weights, tile_dst, tile_src, tile_count, w_self, w_neigh, bias, grad_hidden
 ):
@@ -396,8 +399,7 @@
     ndst = grad_hidden.shape[0] * lax.axis_size("feat")
     moved = arrange(feats, w_self, w_neigh, grad_hidden.shape[0])
     aggregated = aggregate(feats, tile_weights[0], tile_dst[0], tile_src[0], tile_count, ndst)
-    hidden, grad_self, grad_neigh, grad_bias = finish(
-        *exchange(moved, aggregated, bias, grad_hidden))
+    hidden, grad_self, grad_neigh, grad_bias = exchange(moved, aggregated, bias, grad_hidden)
     return (hidden, grad_self, grad_neigh, grad_bias[0])
 
 

time: 77.6 us -> 75.3 us (0.970)
  Pallas kernels: 67.6 us -> 65.4 us
    pallas_call x1, Pallas kernels: 49.1 us -> 47.5 us  [exchange(): pl.pallas_call(functools.partial(exchange_kernel, groups, nfeat), out_sha...]
    pallas_call x2 -> x1, Pallas kernels: 16 us -> 15.5 us  [aggregate(): pl.pallas_call(aggregate_kernel, in_specs=[smem, smem, smem, any_spec, an...]
    unnamed x16 -> x12, local copies, waits for them, and re-layouts: 3.72 us -> 3.76 us
  transfers between devices with their start and end apart: 3 -> 3, of which waited for: 0 -> 0; matrix products, arithmetic and copies ran while one was open for 0% -> 0% of each run, Pallas kernels for 18% -> 21%
where the time goes in v7:
time: 75.3 us; the launch traced here: 75.1 us
  Pallas kernels  65.4 us (87%)
  starting transfers between devices  4.55 us (6%)
  local copies, waits for them, and re-layouts  3.76 us (5%)
  between operations  1.38 us (2%)
    pallas_call x1, Pallas kernels, exchange(): pl.pallas_call(functools.partial(exchange_kernel, groups, nfeat), out_sha...  47.5 us
    pallas_call x1, Pallas kernels, aggregate(): pl.pallas_call(aggregate_kernel, in_specs=[smem, smem, smem, any_spec, an...  15.5 us
    ppermute x3, starting transfers between devices, arrange(): lax.ppermute(pieces[p], 'feat', [(f, f ^ 2 * p) for f in range(nfeat)])  4.55 us
    unnamed x12, local copies, waits for them, and re-layouts  3.76 us
    pallas_call x1, Pallas kernels, arrange(): pl.pallas_call(functools.partial(arrange_kernel, outer), out_shape=(jax.S...  2.43 us
  transfers between devices with their start and end apart: 3, of which 0 were waited for; matrix products, arithmetic and copies ran while one was open for 0% of the time, Pallas kernels for 21%

profile of v7, /device:TPU:0, one launch (start us, length us, event | category | flops | bytes accessed | tf_op | source)
XLA Modules:
  0.0 75.1 jit_solution(858296690454674071)
XLA Ops:
  0.6 0.0 copy-start.2
  0.6 0.0 copy-start.3
  0.7 2.4 %arrange.1 = (bf16[320,512]{1,0:T(8,128)(2,1)}, bf16[320,512]{1,0:T(8,128)(2,1)}, bf16[320,512]{1,0:T(8,128)(2,1)}, bf16[320,512]{1,0:T(8,128)(2,1)}) custom-call(bf16[64,256]{1,0:T(8,128)(2,1)} %ws_ref.1, bf16[64,256]{1,0:T(8,128)(2,1)} %wn_ref.1, bf16[64,16384]{1,0:T(8,128)(2,1)} %bitcast.8, bf16[64,16384]{1,0:T(8,128)(2,1)} %bitcast.9, ...), custom_call_target="tpu_custom_call" | custom-call | tf_op jit(solution)/shard_map/arrange/pallas_call | solution.py:124
  3.1 0.0 copy-start.1
  3.1 3.0 %collective-permute-start = (bf16[320,512]{1,0:T(8,128)(2,1)}, bf16[320,512]{1,0:T(8,128)(2,1)S(1)}, u32[]{:S(2)}, u32[]{:S(2)}) collective-permute-start(bf16[320,512]{1,0:T(8,128)(2,1)} %get-tuple-element.13), channel_id=1, source_target_pairs={{0,2},{1,3},{2,0},{3,1},{4,6},{5,7},{6,4},{7,5},{8,10},{9,11},{10,... | collective-permute-start | bytes 983048 | tf_op jit(solution)/shard_map/ppermute | solution.py:137
  6.1 1.6 %collective-permute-start.1 = (bf16[320,512]{1,0:T(8,128)(2,1)}, bf16[320,512]{1,0:T(8,128)(2,1)S(1)}, u32[]{:S(2)}, u32[]{:S(2)}) collective-permute-start(bf16[320,512]{1,0:T(8,128)(2,1)} %get-tuple-element.14), channel_id=1, source_target_pairs={{0,4},{1,5},{2,6},{3,7},{4,0},{5,1},{6,2},{7,3},{8,12},{9,13},{10,... | collective-permute-start | bytes 983048 | tf_op jit(solution)/shard_map/ppermute | solution.py:137
  7.6 0.0 collective-permute-start.2
  8.3 15.5 %aggregate.1.refs_4_ = bf16[64,8192]{1,0:T(8,128)(2,1)} custom-call(s32[512]{0:T(512)} %bitcast.14, s32[512]{0:T(512)} %bitcast.15, s32[1]{0:T(128)S(6)} %copy.17.count_ref, bf16[64,16384]{1,0:T(8,128)(2,1)} %bitcast.12, bf16[512,128,128]{2,1,0:T(8,128)(2,1)} %bitcast.13), custom_call_target="tpu_custom_call" | custom-call | flops 1073741824 | bytes 16777216 | tf_op jit(solution)/shard_map/aggregate/pallas_call | solution.py:71
  23.8 0.0 collective-permute-done.refs_1_
  23.8 0.0 collective-permute-done.1.refs_2_
  23.8 0.0 collective-permute-done.2.refs_3_
  23.8 0.0 copy-done.2
  23.8 0.0 copy-done.3
  23.8 0.0 copy-done.1
  23.8 0.0 copy-start
  23.8 1.2 %copy-done = bf16[64,8192]{1,0:T(8,128)(2,1)S(1)} copy-done((bf16[64,8192]{1,0:T(8,128)(2,1)S(1)}, bf16[64,8192]{1,0:T(8,128)(2,1)}, u32[]{:S(2)}) %copy-start) | copy-done | bytes 1048600
  25.1 47.5 %exchange.1 = (bf16[512,256]{1,0:T(8,128)(2,1)S(1)}, f32[64,256]{1,0:T(8,128)S(1)}, f32[64,256]{1,0:T(8,128)S(1)}, f32[1,256]{1,0:T(1,128)S(1)}) custom-call(bf16[320,512]{1,0:T(8,128)(2,1)S(1)} %copy-done.1, bf16[320,512]{1,0:T(8,128)(2,1)S(1)} %collective-permute-done.refs_1_, bf16[320,512]{1,0:T(8,128)(2,1)S(1)} %collective-permute-done.1.refs_2_, ...), custom_call_target="tpu_custom_call" | custom-call | tf_op jit(solution)/shard_map/exchange/pallas_call | solution.py:355
  72.6 0.7 copy.18
  73.3 0.6 copy.19
  73.9 0.6 copy.20
  74.5 0.6 copy.21
Async XLA Ops:
  0.6 23.2 %copy-start.2 = (bf16[512,256]{1,0:T(8,128)(2,1)S(1)}, bf16[512,256]{1,0:T(8,128)(2,1)}, u32[]{:S(2)}) copy-start(bf16[512,256]{1,0:T(8,128)(2,1)} %refs_6_.1) | copy-start | bytes 786436
  0.6 23.2 %copy-start.3 = (f32[256]{0:T(256)S(1)}, f32[256]{0:T(256)}, u32[]{:S(2)}) copy-start(f32[256]{0:T(256)} %param.16) | copy-start | bytes 3076
  3.1 20.7 %copy-start.1 = (bf16[320,512]{1,0:T(8,128)(2,1)S(1)}, bf16[320,512]{1,0:T(8,128)(2,1)}, u32[]{:S(2)}) copy-start(bf16[320,512]{1,0:T(8,128)(2,1)} %get-tuple-element.12.refs_0_) | copy-start | bytes 983044
  3.1 20.7 %collective-permute-start = (bf16[320,512]{1,0:T(8,128)(2,1)}, bf16[320,512]{1,0:T(8,128)(2,1)S(1)}, u32[]{:S(2)}, u32[]{:S(2)}) collective-permute-start(bf16[320,512]{1,0:T(8,128)(2,1)} %get-tuple-element.13), channel_id=1, source_target_pairs={{0,2},{1,3},{2,0},{3,1},{4,6},{5,7},{6,4},{7,5},{8,10},{9,11},{10,... | collective-permute-start | bytes 983048 | tf_op jit(solution)/shard_map/ppermute | solution.py:137
  6.1 17.7 %collective-permute-start.1 = (bf16[320,512]{1,0:T(8,128)(2,1)}, bf16[320,512]{1,0:T(8,128)(2,1)S(1)}, u32[]{:S(2)}, u32[]{:S(2)}) collective-permute-start(bf16[320,512]{1,0:T(8,128)(2,1)} %get-tuple-element.14), channel_id=1, source_target_pairs={{0,4},{1,5},{2,6},{3,7},{4,0},{5,1},{6,2},{7,3},{8,12},{9,13},{10,... | collective-permute-start | bytes 983048 | tf_op jit(solution)/shard_map/ppermute | solution.py:137
  7.6 16.2 %collective-permute-start.2 = (bf16[320,512]{1,0:T(8,128)(2,1)}, bf16[320,512]{1,0:T(8,128)(2,1)S(1)}, u32[]{:S(2)}, u32[]{:S(2)}) collective-permute-start(bf16[320,512]{1,0:T(8,128)(2,1)} %get-tuple-element.15), channel_id=1, source_target_pairs={{0,6},{1,7},{2,4},{3,5},{4,2},{5,3},{6,0},{7,1},{8,14},{9,15},{10,... | collective-permute-start | bytes 983048 | tf_op jit(solution)/shard_map/ppermute | solution.py:137
  23.8 1.2 %copy-start = (bf16[64,8192]{1,0:T(8,128)(2,1)S(1)}, bf16[64,8192]{1,0:T(8,128)(2,1)}, u32[]{:S(2)}) copy-start(bf16[64,8192]{1,0:T(8,128)(2,1)} %aggregate.1.refs_4_) | copy-start | bytes 3145732

commit v8 on v7

--- a/solution.py
+++ b/solution.py
@@ -7,44 +7,31 @@
 from jax.experimental.pallas import tpu as pltpu
 from jax.sharding import PartitionSpec as P
 
-STEP = 32
+STREAMS = 4
+BATCH = 16
+STEP = STREAMS * BATCH
 PACK = 16
 
 
-def aggregate_kernel(
-    dst_ref, src_ref, count_ref, x_any, w_any, out_ref, x_ref, w_ref, acc_a, acc_b, x_sems, w_sems
-):
-    fcols = x_any.shape[0]
-    total, tile, _ = w_any.shape
+def aggregate_kernel(dst_ref, src_ref, count_ref, x_ref, *refs):
+    w_refs = refs[:STREAMS]
+    out_ref, acc_a, acc_b = refs[STREAMS:]
+    step = pl.program_id(0)
+    fcols = x_ref.shape[0]
+    tile = w_refs[0].shape[1]
     dtiles = out_ref.shape[1] // tile
 
-    x_copies = [
-        pltpu.make_async_copy(
-            x_any.at[pl.ds(q * PACK, PACK)], x_ref.at[pl.ds(q * PACK, PACK)], x_sems.at[q])
-        for q in range(fcols // PACK)
-    ]
-
-    def w_copy(step):
-        span = pl.ds(step * STEP, STEP)
-        return pltpu.make_async_copy(w_any.at[span], w_ref.at[span], w_sems.at[step])
-
-    for copy in x_copies:
-        copy.start()
-    for step in range(total // STEP):
-        w_copy(step).start()
-    acc_a[...] = jnp.zeros_like(acc_a)
-    acc_b[...] = jnp.zeros_like(acc_b)
-    for copy in x_copies:
-        copy.wait()
+    @pl.when(step == 0)
+    def _():
+        acc_a[...] = jnp.zeros_like(acc_a)
+        acc_b[...] = jnp.zeros_like(acc_b)
 
     def place(t):
         return jnp.where(t < count_ref[0], dst_ref[t], dtiles)
 
-    @pl.loop(0, total // STEP)
-    def _(step):
-        w_copy(step).wait()
-        for k in range(0, STEP, 2):
-            t = step * STEP + k
+    for q, w_ref in enumerate(w_refs):
+        for k in range(0, BATCH, 2):
+            t = step * STEP + q * BATCH + k
             one, two = [
                 x_ref[:, pl.ds(pl.multiple_of(src_ref[t + n] * tile, tile), tile)]
                 for n in range(2)
@@ -52,34 +39,36 @@
             zero = jnp.zeros_like(one)
             left = jnp.concatenate([
                 jnp.concatenate([one, zero], axis=1), jnp.concatenate([zero, two], axis=1)], axis=0)
-            right = jnp.concatenate([w_ref[t], w_ref[t + 1]], axis=1)
+            right = jnp.concatenate([w_ref[k], w_ref[k + 1]], axis=1)
             prod = lax.dot_general(
                 left, right, (((1,), (1,)), ((), ())), preferred_element_type=jnp.float32)
             a, b = place(t), place(t + 1)
             acc_a[a] = acc_a[a] + prod[:fcols]
             acc_b[b] = acc_b[b] + prod[fcols:]
 
-    for d in range(dtiles):
-        out_ref[:, d * tile:(d + 1) * tile] = (acc_a[d] + acc_b[d]).astype(out_ref.dtype)
+    @pl.when(step == pl.num_programs(0) - 1)
+    def _():
+        for d in range(dtiles):
+            out_ref[:, d * tile:(d + 1) * tile] = (acc_a[d] + acc_b[d]).astype(out_ref.dtype)
 
 
 def aggregate(feats, tiles, dsts, srcs, count, ndst):
     fcols, nsrc = feats.shape
     total, tile, _ = tiles.shape
-    smem = pl.BlockSpec(memory_space=pltpu.SMEM)
-    any_spec = pl.BlockSpec(memory_space=pl.ANY)
     return pl.pallas_call(
         aggregate_kernel,
-        in_specs=[smem, smem, smem, any_spec, any_spec],
-        out_specs=pl.BlockSpec(memory_space=pltpu.VMEM),
-        scratch_shapes=[
-            pltpu.VMEM((fcols, nsrc), jnp.bfloat16),
-            pltpu.VMEM((total, tile, tile), jnp.bfloat16),
-            pltpu.VMEM((ndst // tile + 1, fcols, tile), jnp.float32),
-            pltpu.VMEM((ndst // tile + 1, fcols, tile), jnp.float32),
-            pltpu.SemaphoreType.DMA((fcols // PACK,)),
-            pltpu.SemaphoreType.DMA((total // STEP,)),
-        ],
+        grid_spec=pltpu.PrefetchScalarGridSpec(
+            num_scalar_prefetch=3,
+            grid=(total // STEP,),
+            in_specs=[
+                pl.BlockSpec((fcols, nsrc), lambda i, *_: (0, 0), pipeline_mode=pl.Buffered(1)),
+            ] + [
+                pl.BlockSpec((BATCH, tile, tile), lambda i, *_, q=q: (i * STREAMS + q, 0, 0))
+                for q in range(STREAMS)
+            ],
+            out_specs=pl.BlockSpec((fcols, ndst), lambda i, *_: (0, 0), pipeline_mode=pl.Buffered(1)),
+            scratch_shapes=[pltpu.VMEM((ndst // tile + 1, fcols, tile), jnp.float32)] * 2,
+        ),
         out_shape=jax.ShapeDtypeStruct((fcols, ndst), jnp.bfloat16),
         compiler_params=pltpu.CompilerParams(vmem_limit_bytes=60 * 2**20),
         cost_estimate=pl.CostEstimate(
@@ -87,7 +76,7 @@
             transcendentals=0,
         ),
         name="aggregate",
-    )(dsts, srcs, count, feats, tiles)
+    )(dsts, srcs, count, feats, *[tiles] * STREAMS)
 
 
 MERGE = 8

time: 75.3 us -> 73.6 us (0.977)
  Pallas kernels: 65.4 us -> 63.3 us
    pallas_call x1, Pallas kernels: 15.5 us -> 13.6 us  [aggregate(): pl.pallas_call(aggregate_kernel, grid_spec=pltpu.PrefetchScalarGridSpec(n...]
  transfers between devices with their start and end apart: 3 -> 3, of which waited for: 0 -> 1; matrix products, arithmetic and copies ran while one was open for 0% -> 0% of each run, Pallas kernels for 21% -> 18%
where the time goes in v8:
time: 73.6 us; the launch traced here: 73.3 us
  Pallas kernels  63.3 us (86%)
  starting transfers between devices  4.55 us (6%)
  local copies, waits for them, and re-layouts  3.76 us (5%)
  between operations  1.34 us (2%)
    pallas_call x1, Pallas kernels, exchange(): pl.pallas_call(functools.partial(exchange_kernel, groups, nfeat), out_sha...  47.4 us
    pallas_call x1, Pallas kernels, aggregate(): pl.pallas_call(aggregate_kernel, grid_spec=pltpu.PrefetchScalarGridSpec(n...  13.6 us
    ppermute x3, starting transfers between devices, arrange(): lax.ppermute(pieces[p], 'feat', [(f, f ^ 2 * p) for f in range(nfeat)])  4.55 us
    unnamed x12, local copies, waits for them, and re-layouts  3.76 us
    pallas_call x1, Pallas kernels, arrange(): pl.pallas_call(functools.partial(arrange_kernel, outer), out_shape=(jax.S...  2.4 us
  transfers between devices with their start and end apart: 3, of which 1 were waited for; matrix products, arithmetic and copies ran while one was open for 0% of the time, Pallas kernels for 18%

profile of v8, /device:TPU:0, one launch (start us, length us, event | category | flops | bytes accessed | tf_op | source)
XLA Modules:
  0.0 73.3 jit_solution(7094568107736136985)
XLA Ops:
  0.6 2.4 %arrange.1 = (bf16[320,512]{1,0:T(8,128)(2,1)}, bf16[320,512]{1,0:T(8,128)(2,1)}, bf16[320,512]{1,0:T(8,128)(2,1)}, bf16[320,512]{1,0:T(8,128)(2,1)}) custom-call(bf16[64,256]{1,0:T(8,128)(2,1)} %ws_ref.1, bf16[64,256]{1,0:T(8,128)(2,1)} %wn_ref.1, bf16[64,16384]{1,0:T(8,128)(2,1)} %bitcast.12, bf16[64,16384]{1,0:T(8,128)(2,1)} %bitcast.13, ...), custom_call_target="tpu_custom_call" | custom-call | tf_op jit(solution)/shard_map/arrange/pallas_call | solution.py:113
  3.0 3.0 %collective-permute-start = (bf16[320,512]{1,0:T(8,128)(2,1)}, bf16[320,512]{1,0:T(8,128)(2,1)S(1)}, u32[]{:S(2)}, u32[]{:S(2)}) collective-permute-start(bf16[320,512]{1,0:T(8,128)(2,1)} %get-tuple-element.13), channel_id=1, source_target_pairs={{0,2},{1,3},{2,0},{3,1},{4,6},{5,7},{6,4},{7,5},{8,10},{9,11},{10,... | collective-permute-start | bytes 983048 | tf_op jit(solution)/shard_map/ppermute | solution.py:126
  6.0 1.6 %collective-permute-start.1 = (bf16[320,512]{1,0:T(8,128)(2,1)}, bf16[320,512]{1,0:T(8,128)(2,1)S(1)}, u32[]{:S(2)}, u32[]{:S(2)}) collective-permute-start(bf16[320,512]{1,0:T(8,128)(2,1)} %get-tuple-element.14), channel_id=1, source_target_pairs={{0,4},{1,5},{2,6},{3,7},{4,0},{5,1},{6,2},{7,3},{8,12},{9,13},{10,... | collective-permute-start | bytes 983048 | tf_op jit(solution)/shard_map/ppermute | solution.py:126
  7.6 0.0 collective-permute-start.2
  8.2 0.0 copy-start.1
  8.2 0.0 copy-start.2
  8.2 0.0 copy-start.3
  8.3 13.6 %aggregate.1.refs_4_ = bf16[64,8192]{1,0:T(8,128)(2,1)} custom-call(s32[512]{0:T(512)} %bitcast.17, s32[512]{0:T(512)} %bitcast.18, s32[1]{0:T(128)S(6)} %copy.17.count_ref, bf16[64,16384]{1,0:T(8,128)(2,1)} %bitcast.16, bf16[512,128,128]{2,1,0:T(8,128)(2,1)} %bitcast.8, bf16[512,128,128]{2,1,0:T(8,128)(2,1)} %bitcast.9, bf16[512,128,128]{2,1,0:T(8,128)(2,1)} %bitcast.10, ...), custom_call_target="tpu_custom_call" | custom-call | flops 1073741824 | bytes 16777216 | tf_op jit(solution)/shard_map/aggregate/pallas_call | solution.py:58
  21.8 0.0 collective-permute-done.refs_1_
  21.8 0.0 collective-permute-done.1.refs_2_
  21.8 0.3 collective-permute-done.2.refs_3_
  22.2 0.0 copy-done.1
  22.2 0.0 copy-done.2
  22.2 0.0 copy-done.3
  22.2 0.0 copy-start
  22.2 1.2 %copy-done = bf16[64,8192]{1,0:T(8,128)(2,1)S(1)} copy-done((bf16[64,8192]{1,0:T(8,128)(2,1)S(1)}, bf16[64,8192]{1,0:T(8,128)(2,1)}, u32[]{:S(2)}) %copy-start) | copy-done | bytes 1048600
  23.4 47.4 %exchange.1 = (bf16[512,256]{1,0:T(8,128)(2,1)S(1)}, f32[64,256]{1,0:T(8,128)S(1)}, f32[64,256]{1,0:T(8,128)S(1)}, f32[1,256]{1,0:T(1,128)S(1)}) custom-call(bf16[320,512]{1,0:T(8,128)(2,1)S(1)} %copy-done.1, bf16[320,512]{1,0:T(8,128)(2,1)S(1)} %collective-permute-done.refs_1_, bf16[320,512]{1,0:T(8,128)(2,1)S(1)} %collective-permute-done.1.refs_2_, ...), custom_call_target="tpu_custom_call" | custom-call | tf_op jit(solution)/shard_map/exchange/pallas_call | solution.py:344
  70.8 0.7 copy.18
  71.5 0.6 copy.19
  72.1 0.6 copy.20
  72.8 0.6 copy.21
Async XLA Ops:
  3.0 18.8 %collective-permute-start = (bf16[320,512]{1,0:T(8,128)(2,1)}, bf16[320,512]{1,0:T(8,128)(2,1)S(1)}, u32[]{:S(2)}, u32[]{:S(2)}) collective-permute-start(bf16[320,512]{1,0:T(8,128)(2,1)} %get-tuple-element.13), channel_id=1, source_target_pairs={{0,2},{1,3},{2,0},{3,1},{4,6},{5,7},{6,4},{7,5},{8,10},{9,11},{10,... | collective-permute-start | bytes 983048 | tf_op jit(solution)/shard_map/ppermute | solution.py:126
  6.0 15.8 %collective-permute-start.1 = (bf16[320,512]{1,0:T(8,128)(2,1)}, bf16[320,512]{1,0:T(8,128)(2,1)S(1)}, u32[]{:S(2)}, u32[]{:S(2)}) collective-permute-start(bf16[320,512]{1,0:T(8,128)(2,1)} %get-tuple-element.14), channel_id=1, source_target_pairs={{0,4},{1,5},{2,6},{3,7},{4,0},{5,1},{6,2},{7,3},{8,12},{9,13},{10,... | collective-permute-start | bytes 983048 | tf_op jit(solution)/shard_map/ppermute | solution.py:126
  7.6 14.6 %collective-permute-start.2 = (bf16[320,512]{1,0:T(8,128)(2,1)}, bf16[320,512]{1,0:T(8,128)(2,1)S(1)}, u32[]{:S(2)}, u32[]{:S(2)}) collective-permute-start(bf16[320,512]{1,0:T(8,128)(2,1)} %get-tuple-element.15), channel_id=1, source_target_pairs={{0,6},{1,7},{2,4},{3,5},{4,2},{5,3},{6,0},{7,1},{8,14},{9,15},{10,... | collective-permute-start | bytes 983048 | tf_op jit(solution)/shard_map/ppermute | solution.py:126
  8.2 13.9 %copy-start.1 = (bf16[320,512]{1,0:T(8,128)(2,1)S(1)}, bf16[320,512]{1,0:T(8,128)(2,1)}, u32[]{:S(2)}) copy-start(bf16[320,512]{1,0:T(8,128)(2,1)} %get-tuple-element.12.refs_0_) | copy-start | bytes 983044
  8.2 13.9 %copy-start.2 = (bf16[512,256]{1,0:T(8,128)(2,1)S(1)}, bf16[512,256]{1,0:T(8,128)(2,1)}, u32[]{:S(2)}) copy-start(bf16[512,256]{1,0:T(8,128)(2,1)} %refs_6_.1) | copy-start | bytes 786436
  8.2 13.9 %copy-start.3 = (f32[256]{0:T(256)S(1)}, f32[256]{0:T(256)}, u32[]{:S(2)}) copy-start(f32[256]{0:T(256)} %param.16) | copy-start | bytes 3076
  22.2 1.2 %copy-start = (bf16[64,8192]{1,0:T(8,128)(2,1)S(1)}, bf16[64,8192]{1,0:T(8,128)(2,1)}, u32[]{:S(2)}) copy-start(bf16[64,8192]{1,0:T(8,128)(2,1)} %aggregate.1.refs_4_) | copy-start | bytes 3145732
